TPU v7x, 32 devices: a whole 2x2x4 slice. The times are simulated.
32 devices in a mesh: fsdp: 32 (over z, y, x, core).
Axes of the slice: x: 2, y: 2, z: 4, core: 2. Of those that a mesh axis runs over, the one named last changes fastest.
Arguments:
- tokens: bfloat16 [16384, 768], P('fsdp'), may hold values from -6 to 6
- lengths: int32 [12], replicated, may hold values from 1 to 2048, 12288 in all
- counts: int32 [32], replicated, may hold values from 256 to 512, as said below
- ln1_gain: bfloat16 [768], P('fsdp'), may hold values from 0.5 to 1.5
- ln1_bias: bfloat16 [768], P('fsdp'), may hold values from -1 to 1
- w_qkv: bfloat16 [768, 2304], P('fsdp'), may hold values from -0.3125 to 0.3125
- bias_q: bfloat16 [768], P('fsdp'), may hold values from -1 to 1
- bias_v: bfloat16 [768], P('fsdp'), may hold values from -1 to 1
- w_out: bfloat16 [768, 768], P('fsdp'), may hold values from -0.875 to 0.875
- bias_out: bfloat16 [768], P('fsdp'), may hold values from -1 to 1
- ln2_gain: bfloat16 [768], P('fsdp'), may hold values from 0.5 to 1.5
- ln2_bias: bfloat16 [768], P('fsdp'), may hold values from -1 to 1
- w_fc: bfloat16 [768, 3072], P('fsdp'), may hold values from -0.21875 to 0.21875
- bias_fc: bfloat16 [3072], P('fsdp'), may hold values from -1 to 1
- w_proj: bfloat16 [3072, 768], P('fsdp'), may hold values from -0.109375 to 0.109375
- bias_proj: bfloat16 [768], P('fsdp'), may hold values from -1 to 1
- grad_out: bfloat16 [16384, 768], P('fsdp'), may hold values from -6 to 6
Outputs:
- activations: bfloat16 [16384, 768], P('fsdp')
- grad_tokens: bfloat16 [16384, 768], P('fsdp')
- grad_ln1_gain: float32 [768], P('fsdp')
- grad_ln1_bias: float32 [768], P('fsdp')
- grad_w_qkv: float32 [768, 2304], P('fsdp')
- grad_bias_q: float32 [768], P('fsdp')
- grad_bias_v: float32 [768], P('fsdp')
- grad_w_out: float32 [768, 768], P('fsdp')
- grad_bias_out: float32 [768], P('fsdp')
- grad_ln2_gain: float32 [768], P('fsdp')
- grad_ln2_bias: float32 [768], P('fsdp')
- grad_w_fc: float32 [768, 3072], P('fsdp')
- grad_bias_fc: float32 [3072], P('fsdp')
- grad_w_proj: float32 [3072, 768], P('fsdp')
- grad_bias_proj: float32 [768], P('fsdp')
Inputs may be any that keep to these rules, and one draw needn't show every extreme that they name: The lengths sum to 12288 and the largest is exactly 2048; the sequences lie one after another over the live slots in device order. Device i holds counts[i] live tokens in its first slots and empty slots after them; the counts sum to 12288; in every draw some device is full and some holds exactly 256.
All inputs are finite; a program needn't handle non-finite values.
Results may differ from a plain program's by a relative error of at most 0.017.
Values may be sent and summed in bfloat16 or wider, within the bound.
A program may use at most 320 MiB of HBM per device.

v0:
```python
import jax
import jax.numpy as jnp
from jax import lax
from jax.sharding import PartitionSpec as P

HD = 64
MAXLEN = 2048


epsilon = 1e-05
masked_out = -1e30


def from_behind(x, axis, by):
    peers = lax.axis_size(axis)
    pairs = [(i, i + by) for i in range(peers) if 0 <= i + by < peers]
    return lax.ppermute(x, axis, pairs)


def layer_norm(values, gain_row, shift_row):
    average = jnp.mean(values, axis=-1, keepdims=True)
    centred = values - average
    variance = jnp.mean(centred * centred, axis=-1, keepdims=True)
    return centred * lax.rsqrt(variance + epsilon) * gain_row + shift_row


def smooth_gelu(values):
    return jax.nn.gelu(values, approximate=True)


def matmul(first_op, second_op):
    return jnp.dot(first_op, second_op, preferred_element_type=jnp.float32)


def times_transposed(first_op, second_op):
    return lax.dot_general(
        first_op, second_op, (((1,), (1,)), ((), ())), preferred_element_type=jnp.float32
    )


def transposed_times(first_op, second_op):
    return lax.dot_general(
        first_op, second_op, (((0,), (0,)), ((), ())), preferred_element_type=jnp.float32
    )


def column_sums(values):
    return jnp.sum(values.astype(jnp.float32), axis=0)


def block_scores(query_heads, key_heads, allowed):
    score_scale = query_heads.shape[2] ** (-0.5)
    raw_scores = (
        jnp.einsum("qhd,khd->hqk", query_heads, key_heads, preferred_element_type=jnp.float32)
        * score_scale
    )
    return jnp.where(allowed[None], raw_scores, masked_out)


def score_grads(query_heads, attn_grads, key_heads, value_heads, allowed, log_total, row_delta):
    scores = block_scores(query_heads, key_heads, allowed)
    softmax_out = jnp.exp(scores - log_total[:, :, None])
    d_softmax = jnp.einsum(
        "qhd,khd->hqk", attn_grads, value_heads, preferred_element_type=jnp.float32
    )
    d_scores = (softmax_out * (d_softmax - row_delta[:, :, None])).astype(jnp.bfloat16)
    return (softmax_out.astype(jnp.bfloat16), d_scores)


def pair_grads(softmax_low, d_scores, query_heads, attn_grads):
    score_scale = query_heads.shape[2] ** (-0.5)
    rows_kept = query_heads.shape[0]
    d_keys = (
        jnp.einsum("hqk,qhd->khd", d_scores, query_heads, preferred_element_type=jnp.float32)
        * score_scale
    )
    d_values = jnp.einsum(
        "hqk,qhd->khd", softmax_low, attn_grads, preferred_element_type=jnp.float32
    )
    return jnp.concatenate([d_keys.reshape(rows_kept, -1), d_values.reshape(rows_kept, -1)], axis=1)


def per_device(
    tokens,
    lengths,
    counts,
    ln1_gain,
    ln1_bias,
    w_qkv,
    bias_q,
    bias_v,
    w_out,
    bias_out,
    ln2_gain,
    ln2_bias,
    w_fc,
    bias_fc,
    w_proj,
    bias_proj,
    grad_out,
):
    (
        gain_one,
        shift_one,
        weight_qkv,
        query_bias,
        value_bias,
        weight_out,
        out_bias,
        gain_two,
        shift_two,
        weight_fc,
        fc_bias,
        weight_proj,
        proj_bias,
    ) = (
        lax.all_gather(ln1_gain, "fsdp", axis=0, tiled=True),
        lax.all_gather(ln1_bias, "fsdp", axis=0, tiled=True),
        lax.all_gather(w_qkv, "fsdp", axis=0, tiled=True),
        lax.all_gather(bias_q, "fsdp", axis=0, tiled=True),
        lax.all_gather(bias_v, "fsdp", axis=0, tiled=True),
        lax.all_gather(w_out, "fsdp", axis=0, tiled=True),
        lax.all_gather(bias_out, "fsdp", axis=0, tiled=True),
        lax.all_gather(ln2_gain, "fsdp", axis=0, tiled=True),
        lax.all_gather(ln2_bias, "fsdp", axis=0, tiled=True),
        lax.all_gather(w_fc, "fsdp", axis=0, tiled=True),
        lax.all_gather(bias_fc, "fsdp", axis=0, tiled=True),
        lax.all_gather(w_proj, "fsdp", axis=0, tiled=True),
        lax.all_gather(bias_proj, "fsdp", axis=0, tiled=True),
    )
    rows_here, features = tokens.shape
    head_count = features // HD
    score_scale = HD ** (-0.5)
    reach_back = (MAXLEN - 2) // (rows_here // 2) + 1
    ndevices = lax.axis_size("fsdp")
    device = lax.axis_index("fsdp")
    total_slots = ndevices * rows_here
    seq_ends = jnp.cumsum(lengths)
    starts = jnp.cumsum(counts) - counts
    offsets = jnp.arange(rows_here, dtype=jnp.int32)

    def slot_info(owner, blank):
        inside = (owner >= 0) & (owner < ndevices)
        safe = jnp.clip(owner, 0, ndevices - 1)
        places = starts[safe] + offsets
        passed = jnp.sum((places[:, None] >= seq_ends[None, :]).astype(jnp.int32), axis=1)
        seq_ids = jnp.where(offsets < counts[safe], passed, -(safe * rows_here + offsets) - 1)
        return (jnp.where(inside, seq_ids, blank), places)

    def allowed_for(query_owner, key_owner):
        query_ids, query_places = slot_info(query_owner, -total_slots - 2)
        key_ids, key_places = slot_info(key_owner, -total_slots - 1)
        return (key_ids[None, :] == query_ids[:, None]) & (
            key_places[None, :] <= query_places[:, None]
        )

    def split_pair(key_value):
        return (
            key_value[:, :features].reshape(rows_here, head_count, HD),
            key_value[:, features:].reshape(rows_here, head_count, HD),
        )

    live = (offsets < counts[device])[:, None]
    inputs = tokens.astype(jnp.float32)
    normed_one = layer_norm(inputs, gain_one.astype(jnp.float32), shift_one.astype(jnp.float32))
    normed_low = normed_one.astype(jnp.bfloat16)
    projected = matmul(normed_low, weight_qkv)
    query = (projected[:, :features] + query_bias.astype(jnp.float32)).astype(jnp.bfloat16)
    pair_bias = jnp.concatenate(
        [jnp.zeros((features,), jnp.float32), value_bias.astype(jnp.float32)]
    )
    key_value = (projected[:, features:] + pair_bias).astype(jnp.bfloat16)
    query_heads = query.reshape(rows_here, head_count, HD)
    local_keys, local_values = split_pair(key_value)
    blocks = [(local_keys, local_values, allowed_for(device, device))]
    for distance in range(1, reach_back + 1):
        far_pair = from_behind(key_value, "fsdp", distance)
        far_keys, far_values = split_pair(far_pair)
        blocks.append((far_keys, far_values, allowed_for(device, device - distance)))
    running_top = jnp.full((head_count, rows_here), masked_out, jnp.float32)
    running_total = jnp.zeros((head_count, rows_here), jnp.float32)
    for key_heads, value_heads, allowed in blocks:
        scores = block_scores(query_heads, key_heads, allowed)
        new_top = jnp.maximum(running_top, jnp.max(scores, axis=2))
        running_total = running_total * jnp.exp(running_top - new_top) + jnp.sum(
            jnp.exp(scores - new_top[:, :, None]), axis=2
        )
        running_top = new_top
    log_total = running_top + jnp.log(running_total)
    attended = jnp.zeros((rows_here, head_count, HD), jnp.float32)
    for key_heads, value_heads, allowed in blocks:
        scores = block_scores(query_heads, key_heads, allowed)
        softmax_low = jnp.exp(scores - log_total[:, :, None]).astype(jnp.bfloat16)
        attended = attended + jnp.einsum(
            "hqk,khd->qhd", softmax_low, value_heads, preferred_element_type=jnp.float32
        )
    mixed_low = attended.reshape(rows_here, features).astype(jnp.bfloat16)
    middle = inputs + matmul(mixed_low, weight_out) + out_bias.astype(jnp.float32)
    normed_two = layer_norm(middle, gain_two.astype(jnp.float32), shift_two.astype(jnp.float32))
    two_low = normed_two.astype(jnp.bfloat16)
    hidden = matmul(two_low, weight_fc) + fc_bias.astype(jnp.float32)
    active, gelu_back = jax.vjp(smooth_gelu, hidden)
    active_low = active.astype(jnp.bfloat16)
    result = middle + matmul(active_low, weight_proj) + proj_bias.astype(jnp.float32)
    activations = jnp.where(live, result, 0.0).astype(jnp.bfloat16)
    (
        gain_one,
        shift_one,
        weight_qkv,
        query_bias,
        value_bias,
        weight_out,
        out_bias,
        gain_two,
        shift_two,
        weight_fc,
        fc_bias,
        weight_proj,
        proj_bias,
    ) = (
        lax.all_gather(ln1_gain, "fsdp", axis=0, tiled=True),
        lax.all_gather(ln1_bias, "fsdp", axis=0, tiled=True),
        lax.all_gather(w_qkv, "fsdp", axis=0, tiled=True),
        lax.all_gather(bias_q, "fsdp", axis=0, tiled=True),
        lax.all_gather(bias_v, "fsdp", axis=0, tiled=True),
        lax.all_gather(w_out, "fsdp", axis=0, tiled=True),
        lax.all_gather(bias_out, "fsdp", axis=0, tiled=True),
        lax.all_gather(ln2_gain, "fsdp", axis=0, tiled=True),
        lax.all_gather(ln2_bias, "fsdp", axis=0, tiled=True),
        lax.all_gather(w_fc, "fsdp", axis=0, tiled=True),
        lax.all_gather(bias_fc, "fsdp", axis=0, tiled=True),
        lax.all_gather(w_proj, "fsdp", axis=0, tiled=True),
        lax.all_gather(bias_proj, "fsdp", axis=0, tiled=True),
    )
    upstream = jnp.where(live, grad_out.astype(jnp.float32), 0.0)
    upstream_low = upstream.astype(jnp.bfloat16)
    grad_w_proj = transposed_times(active_low, upstream_low)
    grad_bias_proj = jnp.sum(upstream, axis=0)
    d_active = times_transposed(upstream_low, weight_proj)
    d_hidden = gelu_back(d_active)[0].astype(jnp.bfloat16)
    grad_w_fc = transposed_times(two_low, d_hidden)
    grad_bias_fc = column_sums(d_hidden)
    d_normed_two = times_transposed(d_hidden, weight_fc)
    unused_two, norm_back_two = jax.vjp(
        layer_norm, middle, gain_two.astype(jnp.float32), shift_two.astype(jnp.float32)
    )
    d_middle_part, grad_ln2_gain, grad_ln2_bias = norm_back_two(d_normed_two)
    d_middle = upstream + d_middle_part
    d_branch = d_middle.astype(jnp.bfloat16)
    grad_w_out = transposed_times(mixed_low, d_branch)
    grad_bias_out = column_sums(d_branch)
    d_attended_flat = times_transposed(d_branch, weight_out).astype(jnp.bfloat16)
    d_attended = d_attended_flat.reshape(rows_here, head_count, HD)
    row_delta = jnp.sum(d_attended.astype(jnp.float32) * attended, axis=2).T
    d_query = jnp.zeros((rows_here, head_count, HD), jnp.float32)
    d_pairs = jnp.zeros((rows_here, 2 * features), jnp.float32)
    for number, (key_heads, value_heads, allowed) in enumerate(blocks):
        softmax_low, d_scores = score_grads(
            query_heads, d_attended, key_heads, value_heads, allowed, log_total, row_delta
        )
        d_query = (
            d_query
            + jnp.einsum("hqk,khd->qhd", d_scores, key_heads, preferred_element_type=jnp.float32)
            * score_scale
        )
        if number == 0:
            d_pairs = pair_grads(softmax_low, d_scores, query_heads, d_attended)
        else:
            d_pair = pair_grads(softmax_low, d_scores, query_heads, d_attended)
            d_pairs = d_pairs + from_behind(d_pair.astype(jnp.bfloat16), "fsdp", -number).astype(
                d_pair.dtype
            )
    d_projected = jnp.concatenate([d_query.reshape(rows_here, features), d_pairs], axis=1).astype(
        jnp.bfloat16
    )
    grad_w_qkv = transposed_times(normed_low, d_projected)
    grad_bias_q = column_sums(d_projected[:, :features])
    grad_bias_v = column_sums(d_projected[:, 2 * features :])
    d_normed_one = times_transposed(d_projected, weight_qkv)
    unused_one, norm_back_one = jax.vjp(
        layer_norm, inputs, gain_one.astype(jnp.float32), shift_one.astype(jnp.float32)
    )
    d_input_part, grad_ln1_gain, grad_ln1_bias = norm_back_one(d_normed_one)
    grad_tokens = (d_middle + d_input_part).astype(jnp.bfloat16)
    owned = tuple(
        (
            lax.psum_scatter(grad_ln1_gain, "fsdp", scatter_dimension=0, tiled=True),
            lax.psum_scatter(grad_ln1_bias, "fsdp", scatter_dimension=0, tiled=True),
            lax.psum_scatter(grad_w_qkv, "fsdp", scatter_dimension=0, tiled=True),
            lax.psum_scatter(grad_bias_q, "fsdp", scatter_dimension=0, tiled=True),
            lax.psum_scatter(grad_bias_v, "fsdp", scatter_dimension=0, tiled=True),
            lax.psum_scatter(grad_w_out, "fsdp", scatter_dimension=0, tiled=True),
            lax.psum_scatter(grad_bias_out, "fsdp", scatter_dimension=0, tiled=True),
            lax.psum_scatter(grad_ln2_gain, "fsdp", scatter_dimension=0, tiled=True),
            lax.psum_scatter(grad_ln2_bias, "fsdp", scatter_dimension=0, tiled=True),
            lax.psum_scatter(grad_w_fc, "fsdp", scatter_dimension=0, tiled=True),
            lax.psum_scatter(grad_bias_fc, "fsdp", scatter_dimension=0, tiled=True),
            lax.psum_scatter(grad_w_proj, "fsdp", scatter_dimension=0, tiled=True),
            lax.psum_scatter(grad_bias_proj, "fsdp", scatter_dimension=0, tiled=True),
        )
    )
    return (activations, grad_tokens) + owned


def solution(mesh):
    return jax.shard_map(
        per_device,
        mesh=mesh,
        in_specs=(
            P("fsdp", None),
            P(),
            P(),
            P("fsdp"),
            P("fsdp"),
            P("fsdp", None),
            P("fsdp"),
            P("fsdp"),
            P("fsdp", None),
            P("fsdp"),
            P("fsdp"),
            P("fsdp"),
            P("fsdp", None),
            P("fsdp"),
            P("fsdp", None),
            P("fsdp"),
            P("fsdp", None),
        ),
        out_specs=(
            P("fsdp", None),
            P("fsdp", None),
            P("fsdp"),
            P("fsdp"),
            P("fsdp", None),
            P("fsdp"),
            P("fsdp"),
            P("fsdp", None),
            P("fsdp"),
            P("fsdp"),
            P("fsdp"),
            P("fsdp", None),
            P("fsdp"),
            P("fsdp", None),
            P("fsdp"),
        ),
        check_vma=False,
    )
```

profile of v0, /device:TPU:0, one launch (start us, length us, event | category | flops | bytes accessed | tf_op | source)
XLA Modules:
  0.0 1469.4 jit_solution(5328969770976692701)
XLA Ops:
  17.6 42.7 %all-reduce.20 = (bf16[768]{0:T(1024)(128)(2,1)S(1)}, bf16[768]{0:T(1024)(128)(2,1)S(1)}, bf16[768]{0:T(1024)(128)(2,1)S(1)}, bf16[768]{0:T(1024)(128)(2,1)S(1)}...) all-reduce(bf16[768]{0:T(1024)(128)(2,1)S(1)} %dynamic-update-slice, ...), channel_id=1, replica_groups=mesh['fsdp'=32] {'fsdp'}, use_global_device_ids=true, to_apply=%add.2 | all-reduce | flops 9216 | bytes 36864
  116.4 13.5 collective-permute-done.7
  132.3 7.6 fusion.9
  141.1 27.9 %collective-permute-start.1 = (bf16[512,1536]{1,0:T(8,128)(2,1)}, bf16[512,1536]{1,0:T(8,128)(2,1)}, u32[]{:S(2)}, u32[]{:S(2)}) collective-permute-start(bf16[512,1536]{1,0:T(8,128)(2,1)} %fusion.25), channel_id=1, source_target_pairs={{0,2},{1,3},{2,4},{3,5},{4,6},{5,7},{6,8},{7,9},{8,10},{9,11},{10,... | collective-permute-start | bytes 4718600 | tf_op jit(solution)/shard_map/ppermute | solution.py:17
  184.9 72.3 %collective-permute-done.3 = bf16[512,1536]{1,0:T(8,128)(2,1)} collective-permute-done((bf16[512,1536]{1,0:T(8,128)(2,1)}, bf16[512,1536]{1,0:T(8,128)(2,1)}, u32[]{:S(2)}, u32[]{:S(2)}) %collective-permute-start.3) | collective-permute-done | bytes 1572896 | tf_op jit(solution)/shard_map/ppermute | solution.py:17
  342.0 7.6 exponential_reduce_fusion.1
  371.1 8.1 exponential_reduce_fusion.5
  379.2 7.7 exponential_reduce_fusion.6
  387.0 7.8 exponential_reduce_fusion.7
  394.8 7.8 exponential_reduce_fusion.8
  416.2 9.1 fusion.71
  429.6 9.0 fusion.77
  438.7 9.1 fusion.80
  451.8 9.0 fusion.83
  478.3 9.9 convert_reduce_fusion
  496.6 7.5 convolution_convert_fusion.1
  504.4 9.4 multiply_convert_fusion.8
  549.3 7.5 convolution_convert_fusion.4
  556.8 8.7 multiply_convert_fusion.3
  572.8 8.6 multiply_convert_fusion.4
  588.6 8.6 multiply_convert_fusion.5
  604.7 8.6 multiply_convert_fusion.6
  620.6 9.1 multiply_convert_fusion.7
  694.5 7.5 fusion.85
  702.0 131.1 %collective-permute-done.15 = bf16[512,1536]{0,1:T(8,128)(2,1)} collective-permute-done((bf16[512,1536]{0,1:T(8,128)(2,1)}, bf16[512,1536]{0,1:T(8,128)(2,1)}, u32[]{:S(2)}, u32[]{:S(2)}) %collective-permute-start.15) | collective-permute-done | bytes 1572896 | tf_op jit(solution)/shard_map/ppermute | solution.py:17
  844.8 33.5 %collective-permute-done.10 = bf16[512,1536]{0,1:T(8,128)(2,1)S(1)} collective-permute-done((bf16[512,1536]{0,1:T(8,128)(2,1)}, bf16[512,1536]{0,1:T(8,128)(2,1)S(1)}, u32[]{:S(2)}, u32[]{:S(2)}) %collective-permute-start.10) | collective-permute-done | bytes 1572896 | tf_op jit(solution)/shard_map/ppermute | solution.py:17
  902.2 10.1 fusion.53
  913.1 9.1 select_convert_fusion
  927.5 207.7 %all-reduce.19 = (f32[768]{0:T(1024)S(1)}, f32[768]{0:T(1024)S(1)}, f32[768]{0:T(1024)S(1)}, f32[768]{0:T(1024)S(1)}, f32[768]{0:T(1024)S(1)}, /*index=5*/f32[76...) all-reduce(f32[768]{0:T(1024)S(1)} %get-tuple-element.17, ...), channel_id=2, replica_groups=mesh['fsdp'=32] {'fsdp'}, use_global_device_ids=true, to_apply=%region_39.40.clone | all-reduce | flops 9216 | bytes 73728
  1140.5 38.2 %reduce-scatter.5.cloned.1.call-done = f32[24,2304]{1,0:T(8,128)} async-done(((f32[768,2304]{1,0:T(8,128)}), f32[24,2304]{1,0:T(8,128)}) %reduce-scatter.5.cloned.1.call-update) | async-done | bytes 221200 | tf_op jit(solution)/shard_map/reduce_scatter | solution.py:289
  1178.7 141.4 %reduce-scatter.9.cloned.1.call-done = f32[24,3072]{1,0:T(8,128)} async-done(((f32[768,3072]{1,0:T(8,128)}), f32[24,3072]{1,0:T(8,128)}) %reduce-scatter.9.cloned.1.call-update) | async-done | bytes 294928 | tf_op jit(solution)/shard_map/reduce_scatter | solution.py:296
  1320.1 142.1 %reduce-scatter.11.cloned.1.call-done = f32[96,768]{1,0:T(8,128)} async-done(((f32[3072,768]{1,0:T(8,128)}), f32[96,768]{1,0:T(8,128)}) %reduce-scatter.11.cloned.1.call-update) | async-done | bytes 294928 | tf_op jit(solution)/shard_map/reduce_scatter | solution.py:298
  (541 shorter events, 415.0 us)
Async XLA Ops:
  7.2 71.2 %all-gather.5.cloned.1.call-start = ((), (), s32[]{:S(2)}) async-start(), calls=%async_computation.4 | async-start | bytes 3649536 | tf_op jit(solution)/shard_map/all_gather | solution.py:119
  7.9 460.2 %all-gather.7.cloned.1.call-start = ((), (), s32[]{:S(2)}) async-start(), calls=%async_computation.5 | async-start | bytes 1216512 | tf_op jit(solution)/shard_map/all_gather | solution.py:122
  8.7 462.3 %all-gather.9.cloned.1.call-start = ((), (), s32[]{:S(2)}) async-start(), calls=%async_computation.6 | async-start | bytes 4866048 | tf_op jit(solution)/shard_map/all_gather | solution.py:126
  9.4 468.8 %all-gather.11.cloned.1.call-start = ((), (), s32[]{:S(2)}) async-start(), calls=%async_computation.7 | async-start | bytes 4866048 | tf_op jit(solution)/shard_map/all_gather | solution.py:128
  10.0 1130.5 %reduce-scatter.7.cloned.1.call-start = ((), (), s32[]{:S(2)}) async-start(), calls=%async_computation.9 | async-start | bytes 2433024 | tf_op jit(solution)/shard_map/reduce_scatter | solution.py:292
  86.4 43.4 %collective-permute-start.7 = (bf16[512,1536]{1,0:T(8,128)(2,1)}, bf16[512,1536]{1,0:T(8,128)(2,1)}, u32[]{:S(2)}, u32[]{:S(2)}) collective-permute-start(bf16[512,1536]{1,0:T(8,128)(2,1)} %fusion.25), channel_id=1, source_target_pairs={{0,8},{1,9},{2,10},{3,11},{4,12},{5,13},{6,14},{7,15},{8,16},{9,17... | collective-permute-start | bytes 4718600 | tf_op jit(solution)/shard_map/ppermute | solution.py:17
  92.3 48.8 %collective-permute-start.6 = (bf16[512,1536]{1,0:T(8,128)(2,1)}, bf16[512,1536]{1,0:T(8,128)(2,1)}, u32[]{:S(2)}, u32[]{:S(2)}) collective-permute-start(bf16[512,1536]{1,0:T(8,128)(2,1)} %fusion.25), channel_id=1, source_target_pairs={{0,7},{1,8},{2,9},{3,10},{4,11},{5,12},{6,13},{7,14},{8,15},{9,16}... | collective-permute-start | bytes 4718600 | tf_op jit(solution)/shard_map/ppermute | solution.py:17
  96.0 76.8 %collective-permute-start.5 = (bf16[512,1536]{1,0:T(8,128)(2,1)}, bf16[512,1536]{1,0:T(8,128)(2,1)}, u32[]{:S(2)}, u32[]{:S(2)}) collective-permute-start(bf16[512,1536]{1,0:T(8,128)(2,1)} %fusion.25), channel_id=1, source_target_pairs={{0,6},{1,7},{2,8},{3,9},{4,10},{5,11},{6,12},{7,13},{8,14},{9,15},... | collective-permute-start | bytes 4718600 | tf_op jit(solution)/shard_map/ppermute | solution.py:17
  105.4 386.2 %copy-start.107 = (f32[768]{0:T(1024)}, f32[768]{0:T(1024)S(1)}, u32[]{:S(2)}) copy-start(f32[768]{0:T(1024)S(1)} %convert_element_type.247) | copy-start | bytes 9220
  105.4 372.8 %copy-start.109 = (f32[3072]{0:T(1024)}, f32[3072]{0:T(1024)S(1)}, u32[]{:S(2)}) copy-start(f32[3072]{0:T(1024)S(1)} %convert_element_type.250) | copy-start | bytes 36868
  106.6 74.5 %collective-permute-start.4 = (bf16[512,1536]{1,0:T(8,128)(2,1)}, bf16[512,1536]{1,0:T(8,128)(2,1)}, u32[]{:S(2)}, u32[]{:S(2)}) collective-permute-start(bf16[512,1536]{1,0:T(8,128)(2,1)} %fusion.25), channel_id=1, source_target_pairs={{0,5},{1,6},{2,7},{3,8},{4,9},{5,10},{6,11},{7,12},{8,13},{9,14},{... | collective-permute-start | bytes 4718600 | tf_op jit(solution)/shard_map/ppermute | solution.py:17
  110.0 147.3 %collective-permute-start.3 = (bf16[512,1536]{1,0:T(8,128)(2,1)}, bf16[512,1536]{1,0:T(8,128)(2,1)}, u32[]{:S(2)}, u32[]{:S(2)}) collective-permute-start(bf16[512,1536]{1,0:T(8,128)(2,1)} %fusion.25), channel_id=1, source_target_pairs={{0,4},{1,5},{2,6},{3,7},{4,8},{5,9},{6,10},{7,11},{8,12},{9,13},{1... | collective-permute-start | bytes 4718600 | tf_op jit(solution)/shard_map/ppermute | solution.py:17
  116.1 216.6 %copy-start = (bf16[512,768]{0,1:T(8,128)(2,1)}, bf16[512,768]{0,1:T(8,128)(2,1)S(1)}, u32[]{:S(2)}) copy-start(bf16[512,768]{0,1:T(8,128)(2,1)S(1)} %copy.267) | copy-start | bytes 2359300
  129.9 130.9 %collective-permute-start.2 = (bf16[512,1536]{1,0:T(8,128)(2,1)}, bf16[512,1536]{1,0:T(8,128)(2,1)}, u32[]{:S(2)}, u32[]{:S(2)}) collective-permute-start(bf16[512,1536]{1,0:T(8,128)(2,1)} %fusion.25), channel_id=1, source_target_pairs={{0,3},{1,4},{2,5},{3,6},{4,7},{5,8},{6,9},{7,10},{8,11},{9,12},{10... | collective-permute-start | bytes 4718600 | tf_op jit(solution)/shard_map/ppermute | solution.py:17
  141.1 123.2 %collective-permute-start.1 = (bf16[512,1536]{1,0:T(8,128)(2,1)}, bf16[512,1536]{1,0:T(8,128)(2,1)}, u32[]{:S(2)}, u32[]{:S(2)}) collective-permute-start(bf16[512,1536]{1,0:T(8,128)(2,1)} %fusion.25), channel_id=1, source_target_pairs={{0,2},{1,3},{2,4},{3,5},{4,6},{5,7},{6,8},{7,9},{8,10},{9,11},{10,... | collective-permute-start | bytes 4718600 | tf_op jit(solution)/shard_map/ppermute | solution.py:17
  172.8 95.1 %collective-permute-start = (bf16[512,1536]{1,0:T(8,128)(2,1)}, bf16[512,1536]{1,0:T(8,128)(2,1)}, u32[]{:S(2)}, u32[]{:S(2)}) collective-permute-start(bf16[512,1536]{1,0:T(8,128)(2,1)} %fusion.25), channel_id=1, source_target_pairs={{0,1},{1,2},{2,3},{3,4},{4,5},{5,6},{6,7},{7,8},{8,9},{9,10},{10,1... | collective-permute-start | bytes 4718600 | tf_op jit(solution)/shard_map/ppermute | solution.py:17
  291.7 169.1 %copy-start.2 = (f32[12,512,512]{1,2,0:T(8,128)}, f32[12,512,512]{1,2,0:T(8,128)S(1)}, u32[]{:S(2)}) copy-start(f32[12,512,512]{1,2,0:T(8,128)S(1)} %get-tuple-element.113) | copy-start | bytes 37748740
  667.9 165.2 %collective-permute-start.15 = (bf16[512,1536]{0,1:T(8,128)(2,1)}, bf16[512,1536]{0,1:T(8,128)(2,1)}, u32[]{:S(2)}, u32[]{:S(2)}) collective-permute-start(bf16[512,1536]{0,1:T(8,128)(2,1)} %pad_maximum_fusion.8), channel_id=1, source_target_pairs={{8,0},{9,1},{10,2},{11,3},{12,4},{13,5},{14,6},{15,7},{16,8},{17,9... | collective-permute-start | bytes 4718600 | tf_op jit(solution)/shard_map/ppermute | solution.py:17
  670.8 163.6 %collective-permute-start.14 = (bf16[512,1536]{0,1:T(8,128)(2,1)}, bf16[512,1536]{0,1:T(8,128)(2,1)}, u32[]{:S(2)}, u32[]{:S(2)}) collective-permute-start(bf16[512,1536]{0,1:T(8,128)(2,1)} %pad_maximum_fusion.7), channel_id=1, source_target_pairs={{7,0},{8,1},{9,2},{10,3},{11,4},{12,5},{13,6},{14,7},{15,8},{16,9}... | collective-permute-start | bytes 4718600 | tf_op jit(solution)/shard_map/ppermute | solution.py:17
  673.6 162.2 %collective-permute-start.13 = (bf16[512,1536]{0,1:T(8,128)(2,1)}, bf16[512,1536]{0,1:T(8,128)(2,1)}, u32[]{:S(2)}, u32[]{:S(2)}) collective-permute-start(bf16[512,1536]{0,1:T(8,128)(2,1)} %pad_maximum_fusion.6), channel_id=1, source_target_pairs={{6,0},{7,1},{8,2},{9,3},{10,4},{11,5},{12,6},{13,7},{14,8},{15,9},... | collective-permute-start | bytes 4718600 | tf_op jit(solution)/shard_map/ppermute | solution.py:17
  676.1 168.6 %collective-permute-start.12 = (bf16[512,1536]{0,1:T(8,128)(2,1)}, bf16[512,1536]{0,1:T(8,128)(2,1)}, u32[]{:S(2)}, u32[]{:S(2)}) collective-permute-start(bf16[512,1536]{0,1:T(8,128)(2,1)} %pad_maximum_fusion.5), channel_id=1, source_target_pairs={{5,0},{6,1},{7,2},{8,3},{9,4},{10,5},{11,6},{12,7},{13,8},{14,9},{... | collective-permute-start | bytes 4718600 | tf_op jit(solution)/shard_map/ppermute | solution.py:17
  678.8 165.9 %collective-permute-start.11 = (bf16[512,1536]{0,1:T(8,128)(2,1)}, bf16[512,1536]{0,1:T(8,128)(2,1)}, u32[]{:S(2)}, u32[]{:S(2)}) collective-permute-start(bf16[512,1536]{0,1:T(8,128)(2,1)} %pad_maximum_fusion.4), channel_id=1, source_target_pairs={{4,0},{5,1},{6,2},{7,3},{8,4},{9,5},{10,6},{11,7},{12,8},{13,9},{1... | collective-permute-start | bytes 4718600 | tf_op jit(solution)/shard_map/ppermute | solution.py:17
  683.1 495.6 %reduce-scatter.5.cloned.1.call-start = ((), (), s32[]{:S(2)}) async-start(), calls=%async_computation.8 | async-start | bytes 7299072 | tf_op jit(solution)/shard_map/reduce_scatter | solution.py:289
  689.5 147.5 %slice-start.3 = ((s8[6291456]{0:T(1024)(128)(4,1)}), s8[4194304]{0:T(1024)(128)(4,1)S(1)}, s32[]{:S(2)}) async-start(s8[6291456]{0:T(1024)(128)(4,1)} %bitcast.231), calls=%async_computation.15 | async-start | bytes 8388608
  689.5 148.8 %slice-start.7 = ((s8[6291456]{0:T(1024)(128)(4,1)}), s8[4194304]{0:T(1024)(128)(4,1)S(1)}, s32[]{:S(2)}) async-start(s8[6291456]{0:T(1024)(128)(4,1)} %bitcast.235), calls=%async_computation.19 | async-start | bytes 8388608
  694.4 142.6 %slice-start.4 = ((s8[6291456]{0:T(1024)(128)(4,1)}), s8[2097152]{0:T(1024)(128)(4,1)S(1)}, s32[]{:S(2)}) async-start(s8[6291456]{0:T(1024)(128)(4,1)} %bitcast.231), calls=%async_computation.16 | async-start | bytes 4194304
  694.5 143.8 %slice-start.8 = ((s8[6291456]{0:T(1024)(128)(4,1)}), s8[2097152]{0:T(1024)(128)(4,1)S(1)}, s32[]{:S(2)}) async-start(s8[6291456]{0:T(1024)(128)(4,1)} %bitcast.235), calls=%async_computation.20 | async-start | bytes 4194304
  833.1 45.1 %collective-permute-start.10 = (bf16[512,1536]{0,1:T(8,128)(2,1)}, bf16[512,1536]{0,1:T(8,128)(2,1)S(1)}, u32[]{:S(2)}, u32[]{:S(2)}) collective-permute-start(bf16[512,1536]{0,1:T(8,128)(2,1)} %pad_maximum_fusion.3), channel_id=1, source_target_pairs={{3,0},{4,1},{5,2},{6,3},{7,4},{8,5},{9,6},{10,7},{11,8},{12,9},{13... | collective-permute-start | bytes 4718600 | tf_op jit(solution)/shard_map/ppermute | solution.py:17
  834.4 46.3 %collective-permute-start.9 = (bf16[512,1536]{0,1:T(8,128)(2,1)}, bf16[512,1536]{0,1:T(8,128)(2,1)}, u32[]{:S(2)}, u32[]{:S(2)}) collective-permute-start(bf16[512,1536]{0,1:T(8,128)(2,1)} %pad_maximum_fusion.2), channel_id=1, source_target_pairs={{2,0},{3,1},{4,2},{5,3},{6,4},{7,5},{8,6},{9,7},{10,8},{11,9},{12,... | collective-permute-start | bytes 4718600 | tf_op jit(solution)/shard_map/ppermute | solution.py:17
  835.7 45.0 %collective-permute-start.8 = (bf16[512,1536]{0,1:T(8,128)(2,1)}, bf16[512,1536]{0,1:T(8,128)(2,1)}, u32[]{:S(2)}, u32[]{:S(2)}) collective-permute-start(bf16[512,1536]{0,1:T(8,128)(2,1)} %pad_maximum_fusion.1), channel_id=1, source_target_pairs={{1,0},{2,1},{3,2},{4,3},{5,4},{6,5},{7,6},{8,7},{9,8},{10,9},{11,1... | collective-permute-start | bytes 4718600 | tf_op jit(solution)/shard_map/ppermute | solution.py:17
  892.9 427.3 %reduce-scatter.9.cloned.1.call-start = ((), (), s32[]{:S(2)}) async-start(), calls=%async_computation.10 | async-start | bytes 9732096 | tf_op jit(solution)/shard_map/reduce_scatter | solution.py:296
  901.5 560.7 %reduce-scatter.11.cloned.1.call-start = ((), (), s32[]{:S(2)}) async-start(), calls=%async_computation.11 | async-start | bytes 9732096 | tf_op jit(solution)/shard_map/reduce_scatter | solution.py:298
  (145 other events, 1731.8 us)
Sparse Core Ops, SparseCore 0:
  10.9 62.9 all-gather.4
  76.8 54.5 all-gather.6
  134.3 133.8 all-gather.8
  270.9 73.9 all-gather.10
  683.2 295.2 reduce-scatter.6
  985.6 193.0 reduce-scatter.4
  1185.2 134.9 reduce-scatter.8
  1327.6 134.5 reduce-scatter.10
where the time goes:
time: 1480 us; the launch traced here: 1470 us
  waiting for transfers between devices  577 us (39%)
  matrix products  373 us (25%)
  blocking collectives  250 us (17%)
  other arithmetic  113 us (8%)
  local copies, waits for them, and re-layouts  76.2 us (5%)
  starting transfers between devices  62.8 us (4%)
  between operations  16.5 us (1%)
    ppermute x16, waiting for transfers between devices, from_behind(): return lax.ppermute(x, axis, pairs)  253 us
    unnamed x2, blocking collectives  250 us
    reduce_scatter x1, waiting for transfers between devices, per_device(): lax.psum_scatter(grad_w_proj, 'fsdp', scatter_dimension=0, tiled=True)  142 us
    reduce_scatter x1, waiting for transfers between devices, per_device(): lax.psum_scatter(grad_w_fc, 'fsdp', scatter_dimension=0, tiled=True)  141 us
    dot_general x9, matrix products, score_grads(): jnp.einsum('qhd,khd->hqk', attn_grads, value_heads, preferred_element_typ...  73.1 us
    dot_general x9, matrix products, pair_grads(): jnp.einsum('hqk,qhd->khd', softmax_low, attn_grads, preferred_element_typ...  66.3 us
    dot_general x9, matrix products, per_device(): jnp.einsum('hqk,khd->qhd', softmax_low, value_heads, preferred_element_ty...  64.3 us
    reduce_sum x9, other arithmetic, per_device(): jnp.sum(jnp.exp(scores - new_top[:, :, None]), axis=2)  63.2 us
  transfers between devices with their start and end apart: 24, of which 8 were waited for; matrix products, arithmetic and copies ran while one was open for 25% of the time, Pallas kernels for 0%

commit v1 on v0

v1 whole, which is shorter than its diff:
```python
import jax
import jax.numpy as jnp
from jax import lax
from jax.experimental import pallas as pl
from jax.experimental.pallas import tpu as pltpu
from jax.sharding import PartitionSpec as P

HD = 64
MAXLEN = 2048
PAIR = 2 * HD
REACH = 8
CHIPS = REACH // 2 + 1
SPOTS = 2 * CHIPS

epsilon = 1e-05
masked_out = -1e30
VMEM_LIMIT = 44 * 1024 * 1024


def layer_norm(values, gain_row, shift_row):
    average = jnp.mean(values, axis=-1, keepdims=True)
    centred = values - average
    variance = jnp.mean(centred * centred, axis=-1, keepdims=True)
    return centred * lax.rsqrt(variance + epsilon) * gain_row + shift_row


def smooth_gelu(values):
    return jax.nn.gelu(values, approximate=True)


def matmul(first_op, second_op):
    return jnp.dot(first_op, second_op, preferred_element_type=jnp.float32)


def times_transposed(first_op, second_op):
    return lax.dot_general(
        first_op, second_op, (((1,), (1,)), ((), ())), preferred_element_type=jnp.float32
    )


def transposed_times(first_op, second_op):
    return lax.dot_general(
        first_op, second_op, (((0,), (0,)), ((), ())), preferred_element_type=jnp.float32
    )


def column_sums(values):
    return jnp.sum(values.astype(jnp.float32), axis=0)


def from_behind(x, by):
    peers = lax.axis_size("fsdp")
    pairs = [(i, i + by) for i in range(peers) if 0 <= i + by < peers]
    return lax.ppermute(x, "fsdp", pairs)


def swap(x, bit):
    peers = lax.axis_size("fsdp")
    return lax.ppermute(x, "fsdp", [(i, i ^ (1 << bit)) for i in range(peers)])


def halves(dtype):
    lane = lax.broadcasted_iota(jnp.int32, (1, PAIR), 1)
    first = (lane < HD).astype(jnp.float32)
    return first.astype(dtype), (1.0 - first).astype(dtype)


def gather_blocks(nb_ref, kv_refs, kv_s, rows):
    far = jnp.maximum(nb_ref[0], nb_ref[1] - 1)
    for e in range(CHIPS):
        low = (SPOTS - 2 - 2 * e) * rows

        def fill(e=e, low=low):
            kv_s[:, low : low + 2 * rows, :] = kv_refs[e][...]

        if e == 0:
            fill()
        else:
            pl.when(far >= 2 * e - 1)(fill)


def forward_kernel(nb_ref, q_ref, *refs):
    kv_refs = refs[:CHIPS]
    lo_ref, hi_ref, code_ref, o_ref, lse_ref, kv_s = refs[CHIPS:]
    rows = q_ref.shape[0] // 2
    gather_blocks(nb_ref, kv_refs, kv_s, rows)
    first, second = halves(jnp.bfloat16)
    first_f, second_f = halves(jnp.float32)
    for qb in range(2):
        q = q_ref[qb * rows : (qb + 1) * rows, :]
        q_heads = (q * first, q * second)
        lo, hi = lo_ref[qb], hi_ref[qb]

        def tile(d, carry, q_heads=q_heads, lo=lo, hi=hi, qb=qb):
            tops, totals, acc = carry
            spot = SPOTS - 2 + qb - d
            at = pl.ds(pl.multiple_of(spot * rows, rows), rows)
            k, v = kv_s[0, at, :], kv_s[1, at, :]
            code = code_ref[spot]
            ok = (code >= lo) & (code <= hi)
            new_tops, new_totals, decays = [], [], []
            gain = None
            for h, v_mask in enumerate((first, second)):
                s = jnp.where(ok, times_transposed(q_heads[h], k), masked_out)
                top = jnp.maximum(tops[h], jnp.max(s, axis=1, keepdims=True))
                p = jnp.exp(s - top)
                decay = jnp.exp(tops[h] - top)
                new_tops.append(top)
                new_totals.append(totals[h] * decay + jnp.sum(p, axis=1, keepdims=True))
                decays.append(decay)
                part = matmul(p.astype(jnp.bfloat16), v * v_mask)
                gain = part if gain is None else gain + part
            acc = acc * (decays[0] * first_f + decays[1] * second_f) + gain
            return tuple(new_tops), tuple(new_totals), acc

        start = jnp.full((rows, 1), masked_out, jnp.float32)
        none = jnp.zeros((rows, 1), jnp.float32)
        tops, totals, acc = lax.fori_loop(
            0,
            nb_ref[qb] + 1,
            tile,
            ((start, start), (none, none), jnp.zeros((rows, PAIR), jnp.float32)),
        )
        here = slice(qb * rows, (qb + 1) * rows)
        o_ref[here, :] = acc / (totals[0] * first_f + totals[1] * second_f)
        lse = [tops[h] + jnp.log(totals[h]) for h in range(2)]
        lse_ref[here, :] = lse[0] * first_f + lse[1] * second_f


def backward_kernel(nb_ref, q_ref, do_ref, *refs):
    kv_refs = refs[:CHIPS]
    lo_ref, hi_ref, code_ref, stat_ref, dq_ref, dkv_ref, kv_s, dk_s, dv_s = refs[CHIPS:]
    rows = q_ref.shape[0] // 2
    gather_blocks(nb_ref, kv_refs, kv_s, rows)
    dk_s[...] = jnp.zeros_like(dk_s)
    dv_s[...] = jnp.zeros_like(dv_s)
    first, second = halves(jnp.bfloat16)
    for qb in range(2):
        here = slice(qb * rows, (qb + 1) * rows)
        q, do = q_ref[here, :], do_ref[here, :]
        q_heads = (q * first, q * second)
        do_heads = (do * first, do * second)
        lo, hi = lo_ref[qb], hi_ref[qb]

        def tile(d, dq_parts, q_heads=q_heads, do_heads=do_heads, lo=lo, hi=hi, qb=qb, here=here):
            spot = SPOTS - 2 + qb - d
            at = pl.ds(pl.multiple_of(spot * rows, rows), rows)
            k, v = kv_s[0, at, :], kv_s[1, at, :]
            k_turned = k.astype(jnp.float32).T.astype(jnp.bfloat16)
            code = code_ref[spot]
            ok = (code >= lo) & (code <= hi)
            new_parts = []
            dk = dv = None
            for h in range(2):
                s = times_transposed(k, q_heads[h])
                p = jnp.where(ok, jnp.exp(s - stat_ref[h : h + 1, here]), 0.0)
                dp = times_transposed(v, do_heads[h])
                ds = (p * (dp - stat_ref[2 + h : 3 + h, here])).astype(jnp.bfloat16)
                dv_part = matmul(p.astype(jnp.bfloat16), do_heads[h])
                dk_part = matmul(ds, q_heads[h])
                dv = dv_part if dv is None else dv + dv_part
                dk = dk_part if dk is None else dk + dk_part
                new_parts.append(dq_parts[h] + matmul(k_turned[h * HD : (h + 1) * HD, :], ds))
            dk_s[at, :] += dk
            dv_s[at, :] += dv
            return tuple(new_parts)

        none = jnp.zeros((HD, rows), jnp.float32)
        parts = lax.fori_loop(0, nb_ref[qb] + 1, tile, (none, none))
        turned = jnp.concatenate(parts, axis=0).T
        dq_ref[here, :] = (turned * HD ** (-0.5)).astype(jnp.bfloat16)
    for e in range(CHIPS):
        low = (SPOTS - 2 - 2 * e) * rows
        dkv_ref[e, 0] = dk_s[low : low + 2 * rows, :].astype(jnp.bfloat16)
        dkv_ref[e, 1] = dv_s[low : low + 2 * rows, :].astype(jnp.bfloat16)


def specs(count):
    return [pl.BlockSpec(memory_space=pltpu.SMEM)] + [pl.BlockSpec(memory_space=pltpu.VMEM)] * (
        count - 1
    )


def attend(nb, q, kvs, lo, hi, code):
    both = q.shape[0]
    operands = (nb, q, *kvs, lo, hi, code)
    out = jax.ShapeDtypeStruct((both, PAIR), jnp.float32)
    return pl.pallas_call(
        forward_kernel,
        out_shape=(out, out),
        in_specs=specs(len(operands)),
        out_specs=(pl.BlockSpec(memory_space=pltpu.VMEM),) * 2,
        scratch_shapes=[pltpu.VMEM((2, CHIPS * both, PAIR), jnp.bfloat16)],
        compiler_params=pltpu.CompilerParams(vmem_limit_bytes=VMEM_LIMIT),
        cost_estimate=pl.CostEstimate(
            flops=8 * both * both * 3 * PAIR, bytes_accessed=8 * both * PAIR * 4, transcendentals=0
        ),
        name="attend",
    )(*operands)


def attend_back(nb, q, do, kvs, lo, hi, code, stats):
    both = q.shape[0]
    operands = (nb, q, do, *kvs, lo, hi, code, stats)
    return pl.pallas_call(
        backward_kernel,
        out_shape=(
            jax.ShapeDtypeStruct((both, PAIR), jnp.bfloat16),
            jax.ShapeDtypeStruct((CHIPS, 2, both, PAIR), jnp.bfloat16),
        ),
        in_specs=specs(len(operands)),
        out_specs=(pl.BlockSpec(memory_space=pltpu.VMEM),) * 2,
        scratch_shapes=[
            pltpu.VMEM((2, CHIPS * both, PAIR), jnp.bfloat16),
            pltpu.VMEM((CHIPS * both, PAIR), jnp.float32),
            pltpu.VMEM((CHIPS * both, PAIR), jnp.float32),
        ],
        compiler_params=pltpu.CompilerParams(vmem_limit_bytes=VMEM_LIMIT),
        cost_estimate=pl.CostEstimate(
            flops=20 * both * both * 3 * PAIR, bytes_accessed=16 * both * PAIR * 4, transcendentals=0
        ),
        name="attend_back",
    )(*operands)


def owner_sums(grads, device, order):
    peers = lax.axis_size("fsdp")
    levels = peers.bit_length() - 1
    width = grads.shape[1]
    held = grads.reshape((2,) * levels + (grads.shape[0] // peers, width))
    left = list(range(levels - 1, -1, -1))
    for bit in list(order) + list(range(len(order), levels)):
        axis = left.index(bit)
        own = (device >> bit) & 1
        sent = lax.dynamic_index_in_dim(held, 1 - own, axis, keepdims=False)
        kept = lax.dynamic_index_in_dim(held, own, axis, keepdims=False)
        held = kept + swap(sent.astype(jnp.bfloat16), bit).astype(jnp.float32)
        left.pop(axis)
    return held


def per_device(
    tokens,
    lengths,
    counts,
    ln1_gain,
    ln1_bias,
    w_qkv,
    bias_q,
    bias_v,
    w_out,
    bias_out,
    ln2_gain,
    ln2_bias,
    w_fc,
    bias_fc,
    w_proj,
    bias_proj,
    grad_out,
):
    rows, features = tokens.shape
    half = features // 2
    pair_count = half // PAIR
    peers = lax.axis_size("fsdp")
    device = lax.axis_index("fsdp")
    core = device % 2

    small_parts = (
        ln1_gain, ln1_bias, bias_q, bias_v, bias_out, ln2_gain, ln2_bias, bias_proj, bias_fc,
    )
    sizes = [part.shape[0] for part in small_parts]
    packed = jnp.concatenate(small_parts).reshape(1, -1)
    packed_all = lax.all_gather(packed, "fsdp", axis=0, tiled=True).astype(jnp.float32)
    weight_qkv = lax.all_gather(w_qkv, "fsdp", axis=0, tiled=True)
    weight_out = lax.all_gather(w_out, "fsdp", axis=0, tiled=True)
    weight_fc = lax.all_gather(w_fc, "fsdp", axis=0, tiled=True)
    weight_proj = lax.all_gather(w_proj, "fsdp", axis=0, tiled=True)
    whole, at = [], 0
    for size in sizes:
        whole.append(packed_all[:, at : at + size].reshape(-1))
        at += size
    (
        gain_one, shift_one, query_bias, value_bias, out_bias, gain_two, shift_two, proj_bias, fc_bias,
    ) = whole

    seq_ends = jnp.cumsum(lengths)
    seq_starts = seq_ends - lengths
    starts = jnp.cumsum(counts) - counts
    offsets = jnp.arange(rows, dtype=jnp.int32)
    total_slots = peers * rows

    def begin_of(places):
        passed = places[..., None] >= seq_ends
        nearest = jnp.max(jnp.where(passed, seq_ends, 0), axis=-1)
        return nearest

    def codes_of(owners):
        safe = jnp.clip(owners, 0, peers - 1)
        places = starts[safe][:, None] + offsets[None, :]
        alive = offsets[None, :] < counts[safe][:, None]
        blank = total_slots + safe[:, None] * rows + offsets[None, :]
        codes = jnp.where(alive, places, blank)
        return codes, jnp.where(alive, begin_of(places), blank)

    first_device = device - core
    near = first_device + jnp.arange(2, dtype=jnp.int32)
    around = first_device - (SPOTS - 2) + jnp.arange(SPOTS, dtype=jnp.int32)
    key_codes = codes_of(around)[0]
    hi, lo = codes_of(near)
    earliest = begin_of(starts[near])
    back = near[:, None] - jnp.arange(1, REACH + 1, dtype=jnp.int32)[None, :]
    back_safe = jnp.clip(back, 0, peers - 1)
    seen = (back >= 0) & (starts[back_safe] + counts[back_safe] > earliest[:, None])
    nb = jnp.sum(seen.astype(jnp.int32), axis=1)
    lo_col, hi_col, code_row = lo[:, :, None], hi[:, :, None], key_codes[:, None, :]
    lo_row, hi_row, code_col = lo[:, None, :], hi[:, None, :], key_codes[:, :, None]

    def trade(x):
        n = x.shape[0]
        cut = x.reshape(n, rows, 2, half)
        mine = lax.dynamic_index_in_dim(cut, core, 2, keepdims=False)
        other = swap(lax.dynamic_index_in_dim(cut, 1 - core, 2, keepdims=False), 0)
        low = jnp.where(core == 0, mine, other)
        high = jnp.where(core == 0, other, mine)
        return jnp.concatenate([low, high], axis=1)

    def trade_back(x):
        mine = lax.dynamic_slice_in_dim(x, core * rows, rows, 1)
        other = swap(lax.dynamic_slice_in_dim(x, (1 - core) * rows, rows, 1), 0)
        low = jnp.where(core == 0, mine, other)
        high = jnp.where(core == 0, other, mine)
        return jnp.concatenate([low, high], axis=2)

    live = (offsets < counts[device])[:, None]
    inputs = tokens.astype(jnp.float32)
    normed_low = layer_norm(inputs, gain_one, shift_one).astype(jnp.bfloat16)
    projected = matmul(normed_low, weight_qkv)
    query = (projected[:, :features] + query_bias).astype(jnp.bfloat16) * jnp.bfloat16(HD ** (-0.5))
    keys = projected[:, features : 2 * features].astype(jnp.bfloat16)
    vals = (projected[:, 2 * features :] + value_bias).astype(jnp.bfloat16)
    traded = trade(jnp.stack([query, keys, vals]))
    queries, blocks, outs, lses = [], [], [], []
    for pair in range(pair_count):
        columns = slice(pair * PAIR, (pair + 1) * PAIR)
        own = traded[1:, :, columns]
        queries.append(traded[0, :, columns])
        blocks.append([own] + [from_behind(own, 2 * e) for e in range(1, CHIPS)])
    for pair in range(pair_count):
        out, lse = attend(nb, queries[pair], blocks[pair], lo_col, hi_col, code_row)
        outs.append(out)
        lses.append(lse)
    attended = jnp.concatenate(outs, axis=1)
    mixed_low = trade_back(attended.astype(jnp.bfloat16)[None])[0]
    middle = inputs + matmul(mixed_low, weight_out) + out_bias
    two_low = layer_norm(middle, gain_two, shift_two).astype(jnp.bfloat16)
    hidden = matmul(two_low, weight_fc) + fc_bias
    active, gelu_back = jax.vjp(smooth_gelu, hidden)
    active_low = active.astype(jnp.bfloat16)
    result = middle + matmul(active_low, weight_proj) + proj_bias
    activations = jnp.where(live, result, 0.0).astype(jnp.bfloat16)

    upstream = jnp.where(live, grad_out.astype(jnp.float32), 0.0)
    upstream_low = upstream.astype(jnp.bfloat16)
    grad_w_proj = transposed_times(active_low, upstream_low)
    grad_bias_proj = jnp.sum(upstream, axis=0)
    d_active = times_transposed(upstream_low, weight_proj)
    d_hidden = gelu_back(d_active)[0].astype(jnp.bfloat16)
    grad_w_fc = transposed_times(two_low, d_hidden)
    grad_bias_fc = column_sums(d_hidden)
    d_normed_two = times_transposed(d_hidden, weight_fc)
    unused_two, norm_back_two = jax.vjp(layer_norm, middle, gain_two, shift_two)
    d_middle_part, grad_ln2_gain, grad_ln2_bias = norm_back_two(d_normed_two)
    d_middle = upstream + d_middle_part
    d_branch = d_middle.astype(jnp.bfloat16)
    grad_w_out = transposed_times(mixed_low, d_branch)
    grad_bias_out = column_sums(d_branch)
    d_attended = trade(times_transposed(d_branch, weight_out).astype(jnp.bfloat16)[None])[0]

    own_proj = owner_sums(grad_w_proj, device, (0, 1, 2))
    own_fc = owner_sums(grad_w_fc, device, (0, 2, 1))
    own_out = owner_sums(grad_w_out, device, (0, 2, 1))

    d_queries, d_pairs = [], []
    for pair in range(pair_count):
        columns = slice(pair * PAIR, (pair + 1) * PAIR)
        d_out = d_attended[:, columns]
        products = d_out.astype(jnp.float32) * outs[pair]
        delta = jnp.sum(products.reshape(2 * rows, 2, HD), axis=2)
        stats = jnp.concatenate([lses[pair][:, ::HD].T, delta.T], axis=0)
        d_query, d_blocks = attend_back(
            nb, queries[pair], d_out, blocks[pair], lo_row, hi_row, code_col, stats
        )
        total = d_blocks[0].astype(jnp.float32)
        for e in range(1, CHIPS):
            total = total + from_behind(d_blocks[e], -2 * e).astype(jnp.float32)
        d_queries.append(d_query)
        d_pairs.append(total.astype(jnp.bfloat16))
    d_heads = jnp.concatenate(
        [jnp.concatenate(d_queries, axis=1)[None], jnp.concatenate(d_pairs, axis=2)], axis=0
    )
    d_slots = trade_back(d_heads)
    d_projected = jnp.concatenate([d_slots[0], d_slots[1], d_slots[2]], axis=1)
    grad_w_qkv = transposed_times(normed_low, d_projected)
    own_qkv = owner_sums(grad_w_qkv, device, (0, 1, 2))
    grad_bias_q = column_sums(d_slots[0])
    grad_bias_v = column_sums(d_slots[2])
    d_normed_one = times_transposed(d_projected, weight_qkv)
    unused_one, norm_back_one = jax.vjp(layer_norm, inputs, gain_one, shift_one)
    d_input_part, grad_ln1_gain, grad_ln1_bias = norm_back_one(d_normed_one)
    grad_tokens = (d_middle + d_input_part).astype(jnp.bfloat16)

    small_grads = (
        grad_ln1_gain, grad_ln1_bias, grad_bias_q, grad_bias_v, grad_bias_out, grad_ln2_gain,
        grad_ln2_bias, grad_bias_proj, grad_bias_fc,
    )
    packed_grads = jnp.concatenate([g.reshape(peers, -1) for g in small_grads], axis=1)
    own_small = lax.psum_scatter(packed_grads, "fsdp", scatter_dimension=0, tiled=True)[0]
    small, at = [], 0
    for size in sizes:
        small.append(own_small[at : at + size])
        at += size
    (
        own_gain_one, own_shift_one, own_bias_q, own_bias_v, own_bias_out, own_gain_two,
        own_shift_two, own_bias_proj, own_bias_fc,
    ) = small
    return (
        activations,
        grad_tokens,
        own_gain_one,
        own_shift_one,
        own_qkv,
        own_bias_q,
        own_bias_v,
        own_out,
        own_bias_out,
        own_gain_two,
        own_shift_two,
        own_fc,
        own_bias_fc,
        own_proj,
        own_bias_proj,
    )


def solution(mesh):
    split_rows, split_flat = P("fsdp", None), P("fsdp")
    return jax.shard_map(
        per_device,
        mesh=mesh,
        in_specs=(
            split_rows, P(), P(),
            split_flat, split_flat, split_rows, split_flat, split_flat, split_rows, split_flat,
            split_flat, split_flat, split_rows, split_flat, split_rows, split_flat, split_rows,
        ),
        out_specs=(
            split_rows, split_rows,
            split_flat, split_flat, split_rows, split_flat, split_flat, split_rows, split_flat,
            split_flat, split_flat, split_rows, split_flat, split_rows, split_flat,
        ),
        check_vma=False,
    )
```

time: 1480 us -> 764 us (0.52)
  waiting for transfers between devices: 577 us -> 237 us
  matrix products: 373 us -> 54.3 us
  blocking collectives: 250 us -> 94.2 us
  starting transfers between devices: 62.8 us -> 188 us
  other arithmetic: 113 us -> 40.3 us
  Pallas kernels: 0 us -> 41.7 us
  local copies, waits for them, and re-layouts: 76.2 us -> 92.9 us
    reduce_scatter x4 -> x0, waiting for transfers between devices: 322 us -> none  [the longest x1 142 us: per_device(): lax.psum_scatter(grad_w_proj, 'fsdp', scatter_dimension=0, tiled=True)]
    dot_general x54 -> x0, matrix products: 308 us -> none  [the longest x9 73.1 us: score_grads(): jnp.einsum('qhd,khd->hqk', attn_grads, value_heads, preferred_element_typ...]
    unnamed x2, blocking collectives: 250 us -> 94.2 us
    ppermute x16 -> x48, starting transfers between devices: 62.3 us -> 188 us  [the longest x24 95.3 us: from_behind(): return lax.ppermute(x, 'fsdp', pairs)]
    ppermute x16 -> x48, waiting for transfers between devices: 253 us -> 155 us  [the longest x24 78.1 us: swap(): return lax.ppermute(x, 'fsdp', [(i, i ^ 1 << bit) for i in range(peers)])]
    all_gather x4, waiting for transfers between devices: 0.06 us -> 79 us  [the longest x1 58.7 us: per_device(): weight_proj = lax.all_gather(w_proj, 'fsdp', axis=0, tiled=True)]
    reduce_sum x11 -> x4, other arithmetic: 63.6 us -> 2.41 us  [the longest x3 2.22 us: per_device(): delta = jnp.sum(products.reshape(2 * rows, 2, HD), axis=2)]
    pallas_call x0 -> x6, Pallas kernels: none -> 41.7 us  [the longest x3 21.8 us: attend_back(): pl.pallas_call(backward_kernel, out_shape=(jax.ShapeDtypeStruct((both, PA...]
  transfers between devices with their start and end apart: 24 -> 52, of which waited for: 8 -> 18; matrix products, arithmetic and copies ran while one was open for 25% -> 18% of each run, Pallas kernels for 0% -> 5%
where the time goes in v1:
time: 764 us; the launch traced here: 765 us
  waiting for transfers between devices  237 us (31%)
  starting transfers between devices  188 us (25%)
  blocking collectives  94.2 us (12%)
  local copies, waits for them, and re-layouts  92.9 us (12%)
  matrix products  54.3 us (7%)
  Pallas kernels  41.7 us (5%)
  other arithmetic  40.3 us (5%)
  between operations  16 us (2%)
    ppermute x24, starting transfers between devices, from_behind(): return lax.ppermute(x, 'fsdp', pairs)  95.3 us
    unnamed x2, blocking collectives  94.2 us
    ppermute x24, starting transfers between devices, swap(): return lax.ppermute(x, 'fsdp', [(i, i ^ 1 << bit) for i in range(peers)])  92.8 us
    ppermute x24, waiting for transfers between devices, swap(): return lax.ppermute(x, 'fsdp', [(i, i ^ 1 << bit) for i in range(peers)])  78.1 us
    ppermute x24, waiting for transfers between devices, from_behind(): return lax.ppermute(x, 'fsdp', pairs)  77.3 us
    all_gather x1, waiting for transfers between devices, per_device(): weight_proj = lax.all_gather(w_proj, 'fsdp', axis=0, tiled=True)  58.7 us
    unnamed x205, local copies, waits for them, and re-layouts  29.9 us
    dot_general x4, matrix products, matmul(): return jnp.dot(first_op, second_op, preferred_element_type=jnp.float32)  24.6 us
  transfers between devices with their start and end apart: 52, of which 18 were waited for; matrix products, arithmetic and copies ran while one was open for 18% of the time, Pallas kernels for 5%

profile of v1, /device:TPU:0, one launch (start us, length us, event | category | flops | bytes accessed | tf_op | source)
XLA Modules:
  0.0 764.6 jit_solution(7671637014747580821)
XLA Ops:
  10.0 6.1 concatenate.44
  16.4 42.4 %all-reduce = bf16[9216]{0:T(1024)(128)(2,1)S(1)} all-reduce(bf16[9216]{0:T(1024)(128)(2,1)S(1)} %dynamic-update-slice), channel_id=2, replica_groups=mesh['fsdp'=32] {'fsdp'}, use_global_device_ids=true, to_apply=%add | all-reduce | flops 9216 | bytes 36864
  62.2 11.5 %all-gather.6.cloned.1.call-done = bf16[768,2304]{1,0:T(8,128)(2,1)} async-done(((bf16[24,2304]{1,0:T(8,128)(2,1)}), bf16[768,2304]{1,0:T(8,128)(2,1)}) %all-gather.6.cloned.1.call-update) | async-done | bytes 3538960 | tf_op jit(solution)/shard_map/all_gather | solution.py:274
  113.0 16.7 %collective-permute-done.10.refs_2_ = bf16[2,1024,128]{2,1,0:T(8,128)(2,1)S(1)} collective-permute-done((bf16[2,1024,128]{2,1,0:T(8,128)(2,1)S(1)}, bf16[2,1024,128]{2,1,0:T(8,128)(2,1)S(1)}, u32[]{:S(2)}, u32[]{:S(2)}) %collective-permute-start.10) | collective-permute-done | bytes 524320 | tf_op jit(solution)/shard_map/ppermute | solution.py:54
  139.8 6.2 collective-permute-start.1
  146.8 12.7 %collective-permute-start.2 = (bf16[2,1024,128]{2,1,0:T(8,128)(2,1)S(1)}, bf16[2,1024,128]{2,1,0:T(8,128)(2,1)S(1)}, u32[]{:S(2)}, u32[]{:S(2)}) collective-permute-start(bf16[2,1024,128]{2,1,0:T(8,128)(2,1)S(1)} %get-tuple-element.74.refs_0_), channel_id=1, source_target_pairs={{0,4},{1,5},{2,6},{3,7},{4,8},{5,9},{6,10},{7,11},{8,12},{9,13},{1... | collective-permute-start | bytes 1572872 | tf_op jit(solution)/shard_map/ppermute | solution.py:54
  159.5 33.3 %collective-permute-start.3 = (bf16[2,1024,128]{2,1,0:T(8,128)(2,1)S(1)}, bf16[2,1024,128]{2,1,0:T(8,128)(2,1)S(1)}, u32[]{:S(2)}, u32[]{:S(2)}) collective-permute-start(bf16[2,1024,128]{2,1,0:T(8,128)(2,1)S(1)} %get-tuple-element.74.refs_0_), channel_id=1, source_target_pairs={{0,6},{1,7},{2,8},{3,9},{4,10},{5,11},{6,12},{7,13},{8,14},{9,15},... | collective-permute-start | bytes 1572872 | tf_op jit(solution)/shard_map/ppermute | solution.py:54
  195.5 6.8 attend.5
  203.1 6.8 attend.4
  211.0 6.3 attend.3
  238.6 8.8 %all-gather.10.cloned.1.call-done = bf16[768,3072]{1,0:T(8,128)(2,1)} async-done(((bf16[24,3072]{1,0:T(8,128)(2,1)}), bf16[768,3072]{1,0:T(8,128)(2,1)}) %all-gather.10.cloned.1.call-update) | async-done | bytes 4718608 | tf_op jit(solution)/shard_map/all_gather | solution.py:276
  247.3 8.1 %fusion.99 = f32[512,3072]{1,0:T(8,128)} fusion(bf16[768,3072]{1,0:T(8,128)(2,1)} %all-gather.10.cloned.1.call-done, f32[512,768]{1,0:T(8,128)} %copy-done.52, f32[768]{0:T(1024)S(1)} %add.617, f32[768]{0:T(1024)S(1)} %mul.218, f32[512]{0:T(512)S(1)} %fusion.83, f32[512]{0:T(512)S(1)} %broadcast_multiply_fusion), kind=kOutput, calls=%fused_computation.277 | convolution fusion | flops 2417885184 | bytes 12593152 | tf_op jit(solution)/shard_map/dot_general | solution.py:32
  255.4 58.7 %all-gather.12.cloned.1.call-done = bf16[3072,768]{1,0:T(8,128)(2,1)} async-done(((bf16[96,768]{1,0:T(8,128)(2,1)}), bf16[3072,768]{1,0:T(8,128)(2,1)}) %all-gather.12.cloned.1.call-update) | async-done | bytes 4718608 | tf_op jit(solution)/shard_map/all_gather | solution.py:277
  314.1 10.0 %convert_reduce_fusion = (f32[3072]{0:T(1024)}, bf16[512,3072]{1,0:T(8,128)(2,1)S(1)}) fusion(f32[512,3072]{1,0:T(8,128)} %fusion.99, f32[3072]{0:T(1024)S(1)} %add.620, bf16[3072,768]{1,0:T(8,128)(2,1)} %all-gather.12.cloned.1.call-done, bf16[512,768]{1,0:T(8,128)(2,1)} %param.33, pred[512]{0:T(512)(128)(4,1)S(1)} %iota_compare_fusion.2), kind=kOutput, calls=%fused_computation.16 | convolution fusion | flops 2453271552 | bytes 14967296 | tf_op jit(solution)/shard_map/dot_general | solution.py:36
  342.8 9.7 %select_convert_fusion = bf16[512,768]{1,0:T(8,128)(2,1)} fusion(f32[512,768]{1,0:T(8,128)S(1)} %copy-done.54, bf16[3072,768]{1,0:T(8,128)(2,1)} %all-gather.12.cloned.1.call-done, f32[768]{0:T(1024)S(1)} %add.626, pred[512]{0:T(512)(128)(4,1)S(1)} %iota_compare_fusion.2, f32[512,3072]{1,0:T(8,128)} %fusion.99, f32[3072]{0:T(1024)S(1)} %add.620), kind=kOutput, calls=%fused_computation.81 | convolution fusion | flops 2433220608 | bytes 13385216 | tf_op jit(solution)/shard_map/dot_general | solution.py:32
  367.6 7.7 %attend_back.5 = (bf16[1024,128]{1,0:T(8,128)(2,1)S(1)}, bf16[5,2,1024,128]{3,2,1,0:T(8,128)(2,1)S(1)}) custom-call(s32[2]{0:T(128)S(1)} %fusion.85.nb_ref, bf16[1024,128]{1,0:T(8,128)(2,1)S(1)} %copy-done.17, bf16[1024,128]{1,0:T(8,128)(2,1)S(1)} %copy-done.22, bf16[2,1024,128]{2,1,0:T(8,128)(2,1)S(1)} %copy-done.10, bf16[2,1024,128]{2,1,0:T(8,128)(2,1)S(1)} %copy-done.28, ...), custom_call_target="tpu_custom_call" | custom-call | flops 8053063680 | bytes 8388608 | tf_op jit(solution)/shard_map/attend_back/pallas_call | solution.py:205
  393.9 7.5 attend_back.4
  402.9 16.8 %collective-permute-start.34 = (bf16[2,2,2,24,768]{4,3,2,1,0:T(8,128)(2,1)S(1)}, bf16[2,2,2,24,768]{4,3,2,1,0:T(8,128)(2,1)S(1)}, u32[]{:S(2)}, u32[]{:S(2)}) collective-permute-start(bf16[2,2,2,24,768]{4,3,2,1,0:T(8,128)(2,1)S(1)} %fusion.67), channel_id=1, source_target_pairs={{0,4},{1,5},{2,6},{3,7},{4,0},{5,1},{6,2},{7,3},{8,12},{9,13},{10,... | collective-permute-start | bytes 884744 | tf_op jit(solution)/shard_map/ppermute | solution.py:59
  419.6 6.7 attend_back.3
  426.5 6.5 collective-permute-done.34
  440.1 20.8 %collective-permute-done.22 = bf16[2,1024,128]{2,1,0:T(8,128)(2,1)S(1)} collective-permute-done((bf16[2,1024,128]{2,1,0:T(8,128)(2,1)S(1)}, bf16[2,1024,128]{2,1,0:T(8,128)(2,1)S(1)}, u32[]{:S(2)}, u32[]{:S(2)}) %collective-permute-start.22) | collective-permute-done | bytes 524320 | tf_op jit(solution)/shard_map/ppermute | solution.py:54
  467.3 39.5 %collective-permute-done.18 = bf16[2,1024,128]{2,1,0:T(8,128)(2,1)S(1)} collective-permute-done((bf16[2,1024,128]{2,1,0:T(8,128)(2,1)S(1)}, bf16[2,1024,128]{2,1,0:T(8,128)(2,1)S(1)}, u32[]{:S(2)}, u32[]{:S(2)}) %collective-permute-start.18) | collective-permute-done | bytes 524320 | tf_op jit(solution)/shard_map/ppermute | solution.py:54
  506.7 12.6 %collective-permute-start.35 = (bf16[2,2,24,768]{3,2,1,0:T(8,128)(2,1)S(1)}, bf16[2,2,24,768]{3,2,1,0:T(8,128)(2,1)S(1)}, u32[]{:S(2)}, u32[]{:S(2)}) collective-permute-start(bf16[2,2,24,768]{3,2,1,0:T(8,128)(2,1)S(1)} %fusion.75), channel_id=1, source_target_pairs={{0,2},{1,3},{2,0},{3,1},{4,6},{5,7},{6,4},{7,5},{8,10},{9,11},{10,... | collective-permute-start | bytes 442376 | tf_op jit(solution)/shard_map/ppermute | solution.py:59
  526.5 33.5 %collective-permute-start.36 = (bf16[2,24,768]{2,1,0:T(8,128)(2,1)S(1)}, bf16[2,24,768]{2,1,0:T(8,128)(2,1)S(1)}, u32[]{:S(2)}, u32[]{:S(2)}) collective-permute-start(bf16[2,24,768]{2,1,0:T(8,128)(2,1)S(1)} %fusion.79), channel_id=1, source_target_pairs={{0,8},{1,9},{2,10},{3,11},{4,12},{5,13},{6,14},{7,15},{8,0},{9,1},... | collective-permute-start | bytes 221192 | tf_op jit(solution)/shard_map/ppermute | solution.py:59
  564.9 16.6 %collective-permute-start.37 = (bf16[24,768]{1,0:T(8,128)(2,1)}, bf16[24,768]{1,0:T(8,128)(2,1)}, u32[]{:S(2)}, u32[]{:S(2)}) collective-permute-start(bf16[24,768]{1,0:T(8,128)(2,1)} %fusion.81), channel_id=1, source_target_pairs={{0,16},{1,17},{2,18},{3,19},{4,20},{5,21},{6,22},{7,23},{8,24},{9,... | collective-permute-start | bytes 110600 | tf_op jit(solution)/shard_map/ppermute | solution.py:59
  614.1 51.7 %all-reduce.1 = f32[32,288]{1,0:T(8,128)} all-reduce(f32[32,288]{1,0:T(8,128)S(1)} %concatenate.57), channel_id=3, replica_groups=mesh['fsdp'=32] {'fsdp'}, use_global_device_ids=true, to_apply=%region_25.26.clone | all-reduce | flops 9216 | bytes 73728
  676.8 23.7 %collective-permute-done.44 = bf16[2,2,2,96,768]{4,3,0,1,2:T(8,128)(2,1)S(1)} collective-permute-done((bf16[2,2,2,96,768]{4,3,0,1,2:T(8,128)(2,1)S(1)}, bf16[2,2,2,96,768]{4,3,0,1,2:T(8,128)(2,1)S(1)}, u32[]{:S(2)}, u32[]{:S(2)}) %collective-permute-start.44) | collective-permute-done | bytes 1179680 | tf_op jit(solution)/shard_map/ppermute | solution.py:59
  705.1 8.1 %collective-permute-done.40 = bf16[2,2,24,3072]{3,2,0,1:T(8,128)(2,1)S(1)} collective-permute-done((bf16[2,2,24,3072]{3,2,0,1:T(8,128)(2,1)S(1)}, bf16[2,2,24,3072]{3,2,0,1:T(8,128)(2,1)S(1)}, u32[]{:S(2)}, u32[]{:S(2)}) %collective-permute-start.40) | collective-permute-done | bytes 589856 | tf_op jit(solution)/shard_map/ppermute | solution.py:59
  721.1 8.7 %collective-permute-done.29 = bf16[2,2,2,24,2304]{4,3,0,1,2:T(8,128)(2,1)S(1)} collective-permute-done((bf16[2,2,2,24,2304]{4,3,0,1,2:T(8,128)(2,1)S(1)}, bf16[2,2,2,24,2304]{4,3,0,1,2:T(8,128)(2,1)S(1)}, u32[]{:S(2)}, u32[]{:S(2)}) %collective-permute-start.29) | collective-permute-done | bytes 884768 | tf_op jit(solution)/shard_map/ppermute | solution.py:59
  734.4 5.7 collective-permute-done.30
  743.5 6.3 collective-permute-done.31
  750.7 6.5 collective-permute-done.32
  (473 shorter events, 225.8 us)
Async XLA Ops:
  7.2 66.6 %all-gather.6.cloned.1.call-start = ((), (), s32[]{:S(2)}) async-start(), calls=%async_computation | async-start | bytes 3649536 | tf_op jit(solution)/shard_map/all_gather | solution.py:274
  7.9 226.6 %all-gather.8.cloned.1.call-start = ((), (), s32[]{:S(2)}) async-start(), calls=%async_computation.1 | async-start | bytes 1216512 | tf_op jit(solution)/shard_map/all_gather | solution.py:275
  8.7 238.6 %all-gather.10.cloned.1.call-start = ((), (), s32[]{:S(2)}) async-start(), calls=%async_computation.2 | async-start | bytes 4866048 | tf_op jit(solution)/shard_map/all_gather | solution.py:276
  9.4 304.7 %all-gather.12.cloned.1.call-start = ((), (), s32[]{:S(2)}) async-start(), calls=%async_computation.3 | async-start | bytes 4866048 | tf_op jit(solution)/shard_map/all_gather | solution.py:277
  94.1 35.6 %collective-permute-start.10 = (bf16[2,1024,128]{2,1,0:T(8,128)(2,1)S(1)}, bf16[2,1024,128]{2,1,0:T(8,128)(2,1)S(1)}, u32[]{:S(2)}, u32[]{:S(2)}) collective-permute-start(bf16[2,1024,128]{2,1,0:T(8,128)(2,1)S(1)} %get-tuple-element.76.refs_0_), channel_id=1, source_target_pairs={{0,4},{1,5},{2,6},{3,7},{4,8},{5,9},{6,10},{7,11},{8,12},{9,13},{1... | collective-permute-start | bytes 1572872 | tf_op jit(solution)/shard_map/ppermute | solution.py:54
  96.8 39.9 %collective-permute-start.11 = (bf16[2,1024,128]{2,1,0:T(8,128)(2,1)S(1)}, bf16[2,1024,128]{2,1,0:T(8,128)(2,1)}, u32[]{:S(2)}, u32[]{:S(2)}) collective-permute-start(bf16[2,1024,128]{2,1,0:T(8,128)(2,1)S(1)} %get-tuple-element.76.refs_0_), channel_id=1, source_target_pairs={{0,6},{1,7},{2,8},{3,9},{4,10},{5,11},{6,12},{7,13},{8,14},{9,15},... | collective-permute-start | bytes 1572872 | tf_op jit(solution)/shard_map/ppermute | solution.py:54
  103.2 36.6 %collective-permute-start.12 = (bf16[2,1024,128]{2,1,0:T(8,128)(2,1)S(1)}, bf16[2,1024,128]{2,1,0:T(8,128)(2,1)}, u32[]{:S(2)}, u32[]{:S(2)}) collective-permute-start(bf16[2,1024,128]{2,1,0:T(8,128)(2,1)S(1)} %get-tuple-element.76.refs_0_), channel_id=1, source_target_pairs={{0,8},{1,9},{2,10},{3,11},{4,12},{5,13},{6,14},{7,15},{8,16},{9,17... | collective-permute-start | bytes 1572872 | tf_op jit(solution)/shard_map/ppermute | solution.py:54
  105.8 40.1 %collective-permute-start.5 = (bf16[2,1024,128]{2,1,0:T(8,128)(2,1)S(1)}, bf16[2,1024,128]{2,1,0:T(8,128)(2,1)S(1)}, u32[]{:S(2)}, u32[]{:S(2)}) collective-permute-start(bf16[2,1024,128]{2,1,0:T(8,128)(2,1)S(1)} %get-tuple-element.75.refs_0_), channel_id=1, source_target_pairs={{0,2},{1,3},{2,4},{3,5},{4,6},{5,7},{6,8},{7,9},{8,10},{9,11},{10,... | collective-permute-start | bytes 1572872 | tf_op jit(solution)/shard_map/ppermute | solution.py:54
  107.5 52.0 %collective-permute-start.6 = (bf16[2,1024,128]{2,1,0:T(8,128)(2,1)S(1)}, bf16[2,1024,128]{2,1,0:T(8,128)(2,1)}, u32[]{:S(2)}, u32[]{:S(2)}) collective-permute-start(bf16[2,1024,128]{2,1,0:T(8,128)(2,1)S(1)} %get-tuple-element.75.refs_0_), channel_id=1, source_target_pairs={{0,4},{1,5},{2,6},{3,7},{4,8},{5,9},{6,10},{7,11},{8,12},{9,13},{1... | collective-permute-start | bytes 1572872 | tf_op jit(solution)/shard_map/ppermute | solution.py:54
  129.7 63.1 %collective-permute-start.7 = (bf16[2,1024,128]{2,1,0:T(8,128)(2,1)S(1)}, bf16[2,1024,128]{2,1,0:T(8,128)(2,1)}, u32[]{:S(2)}, u32[]{:S(2)}) collective-permute-start(bf16[2,1024,128]{2,1,0:T(8,128)(2,1)S(1)} %get-tuple-element.75.refs_0_), channel_id=1, source_target_pairs={{0,6},{1,7},{2,8},{3,9},{4,10},{5,11},{6,12},{7,13},{8,14},{9,15},... | collective-permute-start | bytes 1572872 | tf_op jit(solution)/shard_map/ppermute | solution.py:54
  136.7 65.7 %collective-permute-start.8 = (bf16[2,1024,128]{2,1,0:T(8,128)(2,1)S(1)}, bf16[2,1024,128]{2,1,0:T(8,128)(2,1)S(1)}, u32[]{:S(2)}, u32[]{:S(2)}) collective-permute-start(bf16[2,1024,128]{2,1,0:T(8,128)(2,1)S(1)} %get-tuple-element.75.refs_0_), channel_id=1, source_target_pairs={{0,8},{1,9},{2,10},{3,11},{4,12},{5,13},{6,14},{7,15},{8,16},{9,17... | collective-permute-start | bytes 1572872 | tf_op jit(solution)/shard_map/ppermute | solution.py:54
  139.8 71.0 %collective-permute-start.1 = (bf16[2,1024,128]{2,1,0:T(8,128)(2,1)S(1)}, bf16[2,1024,128]{2,1,0:T(8,128)(2,1)S(1)}, u32[]{:S(2)}, u32[]{:S(2)}) collective-permute-start(bf16[2,1024,128]{2,1,0:T(8,128)(2,1)S(1)} %get-tuple-element.74.refs_0_), channel_id=1, source_target_pairs={{0,2},{1,3},{2,4},{3,5},{4,6},{5,7},{6,8},{7,9},{8,10},{9,11},{10,... | collective-permute-start | bytes 1572872 | tf_op jit(solution)/shard_map/ppermute | solution.py:54
  146.8 64.0 %collective-permute-start.2 = (bf16[2,1024,128]{2,1,0:T(8,128)(2,1)S(1)}, bf16[2,1024,128]{2,1,0:T(8,128)(2,1)S(1)}, u32[]{:S(2)}, u32[]{:S(2)}) collective-permute-start(bf16[2,1024,128]{2,1,0:T(8,128)(2,1)S(1)} %get-tuple-element.74.refs_0_), channel_id=1, source_target_pairs={{0,4},{1,5},{2,6},{3,7},{4,8},{5,9},{6,10},{7,11},{8,12},{9,13},{1... | collective-permute-start | bytes 1572872 | tf_op jit(solution)/shard_map/ppermute | solution.py:54
  159.5 51.3 %collective-permute-start.3 = (bf16[2,1024,128]{2,1,0:T(8,128)(2,1)S(1)}, bf16[2,1024,128]{2,1,0:T(8,128)(2,1)S(1)}, u32[]{:S(2)}, u32[]{:S(2)}) collective-permute-start(bf16[2,1024,128]{2,1,0:T(8,128)(2,1)S(1)} %get-tuple-element.74.refs_0_), channel_id=1, source_target_pairs={{0,6},{1,7},{2,8},{3,9},{4,10},{5,11},{6,12},{7,13},{8,14},{9,15},... | collective-permute-start | bytes 1572872 | tf_op jit(solution)/shard_map/ppermute | solution.py:54
  342.6 58.9 %collective-permute-start.33 = (bf16[2,2,2,2,24,768]{5,4,3,2,1,0:T(8,128)(2,1)}, bf16[2,2,2,2,24,768]{5,4,3,2,1,0:T(8,128)(2,1)}, u32[]{:S(2)}, u32[]{:S(2)}) collective-permute-start(bf16[2,2,2,2,24,768]{5,4,3,2,1,0:T(8,128)(2,1)} %fusion.53), channel_id=1, source_target_pairs={{0,1},{1,0},{2,3},{3,2},{4,5},{5,4},{6,7},{7,6},{8,9},{9,8},{10,11... | collective-permute-start | bytes 1769480 | tf_op jit(solution)/shard_map/ppermute | solution.py:59
  378.2 56.2 %collective-permute-start.26 = (bf16[2,1024,128]{2,1,0:T(8,128)(2,1)}, bf16[2,1024,128]{2,1,0:T(8,128)(2,1)}, u32[]{:S(2)}, u32[]{:S(2)}) collective-permute-start(bf16[2,1024,128]{2,1,0:T(8,128)(2,1)} %get-tuple-element.69), channel_id=1, source_target_pairs={{8,0},{9,1},{10,2},{11,3},{12,4},{13,5},{14,6},{15,7},{16,8},{17,9... | collective-permute-start | bytes 1572872 | tf_op jit(solution)/shard_map/ppermute | solution.py:54
  379.7 56.1 %collective-permute-start.25 = (bf16[2,1024,128]{2,1,0:T(8,128)(2,1)}, bf16[2,1024,128]{2,1,0:T(8,128)(2,1)}, u32[]{:S(2)}, u32[]{:S(2)}) collective-permute-start(bf16[2,1024,128]{2,1,0:T(8,128)(2,1)} %get-tuple-element.70), channel_id=1, source_target_pairs={{6,0},{7,1},{8,2},{9,3},{10,4},{11,5},{12,6},{13,7},{14,8},{15,9},... | collective-permute-start | bytes 1572872 | tf_op jit(solution)/shard_map/ppermute | solution.py:54
  381.0 56.4 %collective-permute-start.24 = (bf16[2,1024,128]{2,1,0:T(8,128)(2,1)}, bf16[2,1024,128]{2,1,0:T(8,128)(2,1)}, u32[]{:S(2)}, u32[]{:S(2)}) collective-permute-start(bf16[2,1024,128]{2,1,0:T(8,128)(2,1)} %get-tuple-element.71), channel_id=1, source_target_pairs={{4,0},{5,1},{6,2},{7,3},{8,4},{9,5},{10,6},{11,7},{12,8},{13,9},{1... | collective-permute-start | bytes 1572872 | tf_op jit(solution)/shard_map/ppermute | solution.py:54
  382.3 56.5 %collective-permute-start.23 = (bf16[2,1024,128]{2,1,0:T(8,128)(2,1)}, bf16[2,1024,128]{2,1,0:T(8,128)(2,1)}, u32[]{:S(2)}, u32[]{:S(2)}) collective-permute-start(bf16[2,1024,128]{2,1,0:T(8,128)(2,1)} %get-tuple-element.68), channel_id=1, source_target_pairs={{2,0},{3,1},{4,2},{5,3},{6,4},{7,5},{8,6},{9,7},{10,8},{11,9},{12,... | collective-permute-start | bytes 1572872 | tf_op jit(solution)/shard_map/ppermute | solution.py:54
  402.9 30.1 %collective-permute-start.34 = (bf16[2,2,2,24,768]{4,3,2,1,0:T(8,128)(2,1)S(1)}, bf16[2,2,2,24,768]{4,3,2,1,0:T(8,128)(2,1)S(1)}, u32[]{:S(2)}, u32[]{:S(2)}) collective-permute-start(bf16[2,2,2,24,768]{4,3,2,1,0:T(8,128)(2,1)S(1)} %fusion.67), channel_id=1, source_target_pairs={{0,4},{1,5},{2,6},{3,7},{4,0},{5,1},{6,2},{7,3},{8,12},{9,13},{10,... | collective-permute-start | bytes 884744 | tf_op jit(solution)/shard_map/ppermute | solution.py:59
  437.4 29.5 %collective-permute-start.19 = (bf16[2,1024,128]{2,1,0:T(8,128)(2,1)S(1)}, bf16[2,1024,128]{2,1,0:T(8,128)(2,1)S(1)}, u32[]{:S(2)}, u32[]{:S(2)}) collective-permute-start(bf16[2,1024,128]{2,1,0:T(8,128)(2,1)S(1)} %get-tuple-element.64), channel_id=1, source_target_pairs={{2,0},{3,1},{4,2},{5,3},{6,4},{7,5},{8,6},{9,7},{10,8},{11,9},{12,... | collective-permute-start | bytes 1572872 | tf_op jit(solution)/shard_map/ppermute | solution.py:54
  438.8 68.0 %collective-permute-start.18 = (bf16[2,1024,128]{2,1,0:T(8,128)(2,1)S(1)}, bf16[2,1024,128]{2,1,0:T(8,128)(2,1)S(1)}, u32[]{:S(2)}, u32[]{:S(2)}) collective-permute-start(bf16[2,1024,128]{2,1,0:T(8,128)(2,1)S(1)} %get-tuple-element.61), channel_id=1, source_target_pairs={{8,0},{9,1},{10,2},{11,3},{12,4},{13,5},{14,6},{15,7},{16,8},{17,9... | collective-permute-start | bytes 1572872 | tf_op jit(solution)/shard_map/ppermute | solution.py:54
  460.9 58.5 %collective-permute-start.17 = (bf16[2,1024,128]{2,1,0:T(8,128)(2,1)S(1)}, bf16[2,1024,128]{2,1,0:T(8,128)(2,1)S(1)}, u32[]{:S(2)}, u32[]{:S(2)}) collective-permute-start(bf16[2,1024,128]{2,1,0:T(8,128)(2,1)S(1)} %get-tuple-element.62), channel_id=1, source_target_pairs={{6,0},{7,1},{8,2},{9,3},{10,4},{11,5},{12,6},{13,7},{14,8},{15,9},... | collective-permute-start | bytes 1572872 | tf_op jit(solution)/shard_map/ppermute | solution.py:54
  462.2 57.2 %collective-permute-start.16 = (bf16[2,1024,128]{2,1,0:T(8,128)(2,1)S(1)}, bf16[2,1024,128]{2,1,0:T(8,128)(2,1)S(1)}, u32[]{:S(2)}, u32[]{:S(2)}) collective-permute-start(bf16[2,1024,128]{2,1,0:T(8,128)(2,1)S(1)} %get-tuple-element.63), channel_id=1, source_target_pairs={{4,0},{5,1},{6,2},{7,3},{8,4},{9,5},{10,6},{11,7},{12,8},{13,9},{1... | collective-permute-start | bytes 1572872 | tf_op jit(solution)/shard_map/ppermute | solution.py:54
  463.5 55.9 %collective-permute-start.15 = (bf16[2,1024,128]{2,1,0:T(8,128)(2,1)S(1)}, bf16[2,1024,128]{2,1,0:T(8,128)(2,1)S(1)}, u32[]{:S(2)}, u32[]{:S(2)}) collective-permute-start(bf16[2,1024,128]{2,1,0:T(8,128)(2,1)S(1)} %get-tuple-element.60), channel_id=1, source_target_pairs={{2,0},{3,1},{4,2},{5,3},{6,4},{7,5},{8,6},{9,7},{10,8},{11,9},{12,... | collective-permute-start | bytes 1572872 | tf_op jit(solution)/shard_map/ppermute | solution.py:54
  466.8 200.5 %collective-permute-start.43 = (bf16[2,2,2,2,96,768]{5,4,0,1,2,3:T(8,128)(2,1)}, bf16[2,2,2,2,96,768]{5,4,0,1,2,3:T(8,128)(2,1)}, u32[]{:S(2)}, u32[]{:S(2)}) collective-permute-start(bf16[2,2,2,2,96,768]{5,4,0,1,2,3:T(8,128)(2,1)} %fusion.12), channel_id=1, source_target_pairs={{0,1},{1,0},{2,3},{3,2},{4,5},{5,4},{6,7},{7,6},{8,9},{9,8},{10,11... | collective-permute-start | bytes 7077896 | tf_op jit(solution)/shard_map/ppermute | solution.py:59
  521.3 68.4 %collective-permute-start.27 = (bf16[3,512,384]{2,1,0:T(8,128)(2,1)}, bf16[3,512,384]{2,1,0:T(8,128)(2,1)S(1)}, u32[]{:S(2)}, u32[]{:S(2)}) collective-permute-start(bf16[3,512,384]{2,1,0:T(8,128)(2,1)} %constant_dynamic-slice_fusion.6), channel_id=1, source_target_pairs={{0,1},{1,0},{2,3},{3,2},{4,5},{5,4},{6,7},{7,6},{8,9},{9,8},{10,11... | collective-permute-start | bytes 3538952 | tf_op jit(solution)/shard_map/ppermute | solution.py:59
  526.5 36.5 %collective-permute-start.36 = (bf16[2,24,768]{2,1,0:T(8,128)(2,1)S(1)}, bf16[2,24,768]{2,1,0:T(8,128)(2,1)S(1)}, u32[]{:S(2)}, u32[]{:S(2)}) collective-permute-start(bf16[2,24,768]{2,1,0:T(8,128)(2,1)S(1)} %fusion.79), channel_id=1, source_target_pairs={{0,8},{1,9},{2,10},{3,11},{4,12},{5,13},{6,14},{7,15},{8,0},{9,1},... | collective-permute-start | bytes 221192 | tf_op jit(solution)/shard_map/ppermute | solution.py:59
  601.8 73.2 %collective-permute-start.39 = (bf16[2,2,2,24,3072]{4,3,0,1,2:T(8,128)(2,1)S(1)}, bf16[2,2,2,24,3072]{4,3,0,1,2:T(8,128)(2,1)}, u32[]{:S(2)}, u32[]{:S(2)}) collective-permute-start(bf16[2,2,2,24,3072]{4,3,0,1,2:T(8,128)(2,1)S(1)} %fusion.26), channel_id=1, source_target_pairs={{0,4},{1,5},{2,6},{3,7},{4,0},{5,1},{6,2},{7,3},{8,12},{9,13},{10,... | collective-permute-start | bytes 3538952 | tf_op jit(solution)/shard_map/ppermute | solution.py:59
  612.5 90.4 %collective-permute-start.28 = (bf16[2,2,2,2,24,2304]{5,4,0,1,2,3:T(8,128)(2,1)S(1)}, bf16[2,2,2,2,24,2304]{5,4,0,1,2,3:T(8,128)(2,1)}, u32[]{:S(2)}, u32[]{:S(2)}) collective-permute-start(bf16[2,2,2,2,24,2304]{5,4,0,1,2,3:T(8,128)(2,1)S(1)} %fusion.15), channel_id=1, source_target_pairs={{0,1},{1,0},{2,3},{3,2},{4,5},{5,4},{6,7},{7,6},{8,9},{9,8},{10,11... | collective-permute-start | bytes 5308424 | tf_op jit(solution)/shard_map/ppermute | solution.py:59
  671.3 29.2 %collective-permute-start.44 = (bf16[2,2,2,96,768]{4,3,0,1,2:T(8,128)(2,1)S(1)}, bf16[2,2,2,96,768]{4,3,0,1,2:T(8,128)(2,1)S(1)}, u32[]{:S(2)}, u32[]{:S(2)}) collective-permute-start(bf16[2,2,2,96,768]{4,3,0,1,2:T(8,128)(2,1)S(1)} %fusion.27), channel_id=1, source_target_pairs={{0,2},{1,3},{2,0},{3,1},{4,6},{5,7},{6,4},{7,5},{8,10},{9,11},{10,... | collective-permute-start | bytes 3538952 | tf_op jit(solution)/shard_map/ppermute | solution.py:59
  676.7 36.5 %collective-permute-start.40 = (bf16[2,2,24,3072]{3,2,0,1:T(8,128)(2,1)S(1)}, bf16[2,2,24,3072]{3,2,0,1:T(8,128)(2,1)S(1)}, u32[]{:S(2)}, u32[]{:S(2)}) collective-permute-start(bf16[2,2,24,3072]{3,2,0,1:T(8,128)(2,1)S(1)} %fusion.54), channel_id=1, source_target_pairs={{0,2},{1,3},{2,0},{3,1},{4,6},{5,7},{6,4},{7,5},{8,10},{9,11},{10,... | collective-permute-start | bytes 1769480 | tf_op jit(solution)/shard_map/ppermute | solution.py:59
  (120 other events, 1802.1 us)
Sparse Core Ops, SparseCore 0:
  10.9 62.8 all-gather.5
  76.7 72.3 all-gather.7
  152.0 95.3 all-gather.9
  250.1 64.0 all-gather.11

commit v2 on v1

--- a/solution.py
+++ b/solution.py
@@ -223,7 +223,18 @@
     )(*operands)
 
 
-def owner_sums(grads, device, order):
+def doubled(held, device):
+    levels = lax.axis_size("fsdp").bit_length() - 1
+    for bit in range(levels):
+        other = swap(held, bit)
+        own = (device >> bit) & 1
+        low = jnp.where(own == 0, held, other)
+        high = jnp.where(own == 0, other, held)
+        held = jnp.concatenate([low, high], axis=0)
+    return held
+
+
+def owner_sums(grads, device, order, sent_as=jnp.bfloat16):
     peers = lax.axis_size("fsdp")
     levels = peers.bit_length() - 1
     width = grads.shape[1]
@@ -234,7 +245,7 @@
         own = (device >> bit) & 1
         sent = lax.dynamic_index_in_dim(held, 1 - own, axis, keepdims=False)
         kept = lax.dynamic_index_in_dim(held, own, axis, keepdims=False)
-        held = kept + swap(sent.astype(jnp.bfloat16), bit).astype(jnp.float32)
+        held = kept + swap(sent.astype(sent_as), bit).astype(jnp.float32)
         left.pop(axis)
     return held
 
@@ -270,7 +281,7 @@
     )
     sizes = [part.shape[0] for part in small_parts]
     packed = jnp.concatenate(small_parts).reshape(1, -1)
-    packed_all = lax.all_gather(packed, "fsdp", axis=0, tiled=True).astype(jnp.float32)
+    packed_all = doubled(packed.astype(jnp.float32), device)
     weight_qkv = lax.all_gather(w_qkv, "fsdp", axis=0, tiled=True)
     weight_out = lax.all_gather(w_out, "fsdp", axis=0, tiled=True)
     weight_fc = lax.all_gather(w_fc, "fsdp", axis=0, tiled=True)
@@ -401,7 +412,14 @@
     d_slots = trade_back(d_heads)
     d_projected = jnp.concatenate([d_slots[0], d_slots[1], d_slots[2]], axis=1)
     grad_w_qkv = transposed_times(normed_low, d_projected)
-    own_qkv = owner_sums(grad_w_qkv, device, (0, 1, 2))
+    middle_column = grad_w_qkv.shape[1] // 2
+    own_qkv = jnp.concatenate(
+        [
+            owner_sums(grad_w_qkv[:, :middle_column], device, (0, 1, 2)),
+            owner_sums(grad_w_qkv[:, middle_column:], device, (0, 2, 1)),
+        ],
+        axis=1,
+    )
     grad_bias_q = column_sums(d_slots[0])
     grad_bias_v = column_sums(d_slots[2])
     d_normed_one = times_transposed(d_projected, weight_qkv)
@@ -414,7 +432,7 @@
         grad_ln2_bias, grad_bias_proj, grad_bias_fc,
     )
     packed_grads = jnp.concatenate([g.reshape(peers, -1) for g in small_grads], axis=1)
-    own_small = lax.psum_scatter(packed_grads, "fsdp", scatter_dimension=0, tiled=True)[0]
+    own_small = owner_sums(packed_grads, device, (0, 1, 2), jnp.float32)[0]
     small, at = [], 0
     for size in sizes:
         small.append(own_small[at : at + size])

time: 764 us -> 734 us (0.961); the launches traced: 765 us -> 727 us
  blocking collectives: 94.2 us -> 0 us
  starting transfers between devices: 188 us -> 256 us
  waiting for transfers between devices: 237 us -> 224 us
    unnamed x2 -> x0, blocking collectives: 94.2 us -> none
    ppermute x24 -> x39, starting transfers between devices: 92.8 us -> 154 us  [swap(): return lax.ppermute(x, 'fsdp', [(i, i ^ 1 << bit) for i in range(peers)])]
    all_gather x1, waiting for transfers between devices: 58.7 us -> 24.6 us  [per_device(): weight_proj = lax.all_gather(w_proj, 'fsdp', axis=0, tiled=True)]
    all_gather x1, waiting for transfers between devices: 11.5 us -> 42.6 us  [per_device(): weight_qkv = lax.all_gather(w_qkv, 'fsdp', axis=0, tiled=True)]
    all_gather x1, waiting for transfers between devices: 8.75 us -> 0.02 us  [per_device(): weight_fc = lax.all_gather(w_fc, 'fsdp', axis=0, tiled=True)]
    reshape x9 -> x0, local copies, waits for them, and re-layouts: 8.29 us -> none  [per_device(): g.reshape(peers, -1)]
    ppermute x24 -> x39, waiting for transfers between devices: 78.1 us -> 80.2 us  [swap(): return lax.ppermute(x, 'fsdp', [(i, i ^ 1 << bit) for i in range(peers)])]
    unnamed x205 -> x255, local copies, waits for them, and re-layouts: 29.9 us -> 31.1 us
  transfers between devices with their start and end apart: 52 -> 67, of which waited for: 18 -> 28; matrix products, arithmetic and copies ran while one was open for 18% -> 17% of each run, Pallas kernels for 5% -> 6%
where the time goes in v2:
time: 734 us; the launch traced here: 727 us
  starting transfers between devices  256 us (35%)
  waiting for transfers between devices  224 us (31%)
  local copies, waits for them, and re-layouts  92.1 us (13%)
  matrix products  51.5 us (7%)
  other arithmetic  45.2 us (6%)
  Pallas kernels  41.6 us (6%)
  between operations  16.4 us (2%)
    ppermute x39, starting transfers between devices, swap(): return lax.ppermute(x, 'fsdp', [(i, i ^ 1 << bit) for i in range(peers)])  154 us
    ppermute x24, starting transfers between devices, from_behind(): return lax.ppermute(x, 'fsdp', pairs)  101 us
    ppermute x39, waiting for transfers between devices, swap(): return lax.ppermute(x, 'fsdp', [(i, i ^ 1 << bit) for i in range(peers)])  80.2 us
    ppermute x24, waiting for transfers between devices, from_behind(): return lax.ppermute(x, 'fsdp', pairs)  74.9 us
    all_gather x1, waiting for transfers between devices, per_device(): weight_qkv = lax.all_gather(w_qkv, 'fsdp', axis=0, tiled=True)  42.6 us
    unnamed x255, local copies, waits for them, and re-layouts  31.1 us
    all_gather x1, waiting for transfers between devices, per_device(): weight_proj = lax.all_gather(w_proj, 'fsdp', axis=0, tiled=True)  24.6 us
    pallas_call x3, Pallas kernels, attend_back(): pl.pallas_call(backward_kernel, out_shape=(jax.ShapeDtypeStruct((both, PA...  21.9 us
  transfers between devices with their start and end apart: 67, of which 28 were waited for; matrix products, arithmetic and copies ran while one was open for 17% of the time, Pallas kernels for 6%

profile of v2, /device:TPU:0, one launch (start us, length us, event | category | flops | bytes accessed | tf_op | source)
XLA Modules:
  0.0 726.9 jit_solution(13863265943721395445)
XLA Ops:
  31.2 42.6 %all-gather.5.cloned.1.call-done = bf16[768,2304]{1,0:T(8,128)(2,1)} async-done(((bf16[24,2304]{1,0:T(8,128)(2,1)}), bf16[768,2304]{1,0:T(8,128)(2,1)}) %all-gather.5.cloned.1.call-update) | async-done | bytes 3538960 | tf_op jit(solution)/shard_map/all_gather | solution.py:285
  73.8 4.2 fusion.120
  109.2 5.4 collective-permute-start.16
  121.2 5.2 collective-permute-start.11
  126.4 17.3 %collective-permute-done.15.refs_2_ = bf16[2,1024,128]{2,1,0:T(8,128)(2,1)S(1)} collective-permute-done((bf16[2,1024,128]{2,1,0:T(8,128)(2,1)S(1)}, bf16[2,1024,128]{2,1,0:T(8,128)(2,1)S(1)}, u32[]{:S(2)}, u32[]{:S(2)}) %collective-permute-start.15) | collective-permute-done | bytes 524320 | tf_op jit(solution)/shard_map/ppermute | solution.py:54
  151.2 6.7 collective-permute-start.6
  158.7 14.7 %collective-permute-start.7 = (bf16[2,1024,128]{2,1,0:T(8,128)(2,1)S(1)}, bf16[2,1024,128]{2,1,0:T(8,128)(2,1)S(1)}, u32[]{:S(2)}, u32[]{:S(2)}) collective-permute-start(bf16[2,1024,128]{2,1,0:T(8,128)(2,1)S(1)} %get-tuple-element.76.refs_0_), channel_id=1, source_target_pairs={{0,4},{1,5},{2,6},{3,7},{4,8},{5,9},{6,10},{7,11},{8,12},{9,13},{1... | collective-permute-start | bytes 1572872 | tf_op jit(solution)/shard_map/ppermute | solution.py:54
  173.4 37.6 %collective-permute-start.8 = (bf16[2,1024,128]{2,1,0:T(8,128)(2,1)S(1)}, bf16[2,1024,128]{2,1,0:T(8,128)(2,1)S(1)}, u32[]{:S(2)}, u32[]{:S(2)}) collective-permute-start(bf16[2,1024,128]{2,1,0:T(8,128)(2,1)S(1)} %get-tuple-element.76.refs_0_), channel_id=1, source_target_pairs={{0,6},{1,7},{2,8},{3,9},{4,10},{5,11},{6,12},{7,13},{8,14},{9,15},... | collective-permute-start | bytes 1572872 | tf_op jit(solution)/shard_map/ppermute | solution.py:54
  212.6 6.9 attend.5
  220.3 6.8 attend.4
  228.1 6.0 attend.3
  255.8 5.6 fusion.124
  264.0 5.8 fusion.62
  269.9 24.6 %all-gather.11.cloned.1.call-done = bf16[3072,768]{1,0:T(8,128)(2,1)} async-done(((bf16[96,768]{1,0:T(8,128)(2,1)}), bf16[3072,768]{1,0:T(8,128)(2,1)}) %all-gather.11.cloned.1.call-update) | async-done | bytes 4718608 | tf_op jit(solution)/shard_map/all_gather | solution.py:288
  294.5 9.9 %convert_reduce_fusion = (f32[3072]{0:T(1024)}, bf16[512,3072]{1,0:T(8,128)(2,1)S(1)}) fusion(f32[512,3072]{1,0:T(8,128)} %copy-done.118, f32[3072]{0:T(1024)S(1)} %add.674, bf16[3072,768]{1,0:T(8,128)(2,1)} %all-gather.11.cloned.1.call-done, bf16[512,768]{1,0:T(8,128)(2,1)} %param.33, pred[512]{0:T(512)(128)(4,1)S(1)} %iota_compare_fusion.2), kind=kOutput, calls=%fused_computation.16 | convolution fusion | flops 2453271552 | bytes 14967296 | tf_op jit(solution)/shard_map/dot_general | solution.py:36
  304.5 5.6 fusion.123
  310.1 5.9 multiply_reduce_fusion
  335.0 4.1 fusion.11
  348.3 7.4 %attend_back.5 = (bf16[1024,128]{1,0:T(8,128)(2,1)S(1)}, bf16[5,2,1024,128]{3,2,1,0:T(8,128)(2,1)S(1)}) custom-call(s32[2]{0:T(128)S(1)} %fusion.110.nb_ref, bf16[1024,128]{1,0:T(8,128)(2,1)S(1)} %copy-done.17, bf16[1024,128]{1,0:T(8,128)(2,1)S(1)} %copy-done.22, bf16[2,1024,128]{2,1,0:T(8,128)(2,1)S(1)} %copy-done.10, bf16[2,1024,128]{2,1,0:T(8,128)(2,1)S(1)} %copy-done.28, ...), custom_call_target="tpu_custom_call" | custom-call | flops 8053063680 | bytes 8388608 | tf_op jit(solution)/shard_map/attend_back/pallas_call | solution.py:205
  373.6 7.8 %attend_back.4 = (bf16[1024,128]{1,0:T(8,128)(2,1)S(1)}, bf16[5,2,1024,128]{3,2,1,0:T(8,128)(2,1)S(1)}) custom-call(s32[2]{0:T(128)S(1)} %fusion.110.nb_ref, bf16[1024,128]{1,0:T(8,128)(2,1)S(1)} %copy-done.15, bf16[1024,128]{1,0:T(8,128)(2,1)S(1)} %copy-done.21, bf16[2,1024,128]{2,1,0:T(8,128)(2,1)S(1)} %copy-done.8, bf16[2,1024,128]{2,1,0:T(8,128)(2,1)S(1)} %copy-done.25, ...), custom_call_target="tpu_custom_call" | custom-call | flops 8053063680 | bytes 8388608 | tf_op jit(solution)/shard_map/attend_back/pallas_call | solution.py:205
  382.9 62.0 %collective-permute-start.49 = (bf16[2,2,2,24,768]{4,3,2,1,0:T(8,128)(2,1)S(1)}, bf16[2,2,2,24,768]{4,3,2,1,0:T(8,128)(2,1)S(1)}, u32[]{:S(2)}, u32[]{:S(2)}) collective-permute-start(bf16[2,2,2,24,768]{4,3,2,1,0:T(8,128)(2,1)S(1)} %fusion.68), channel_id=1, source_target_pairs={{0,4},{1,5},{2,6},{3,7},{4,0},{5,1},{6,2},{7,3},{8,12},{9,13},{10,... | collective-permute-start | bytes 884744 | tf_op jit(solution)/shard_map/ppermute | solution.py:59
  444.9 6.7 attend_back.3
  460.5 19.5 %collective-permute-done.27 = bf16[2,1024,128]{2,1,0:T(8,128)(2,1)S(1)} collective-permute-done((bf16[2,1024,128]{2,1,0:T(8,128)(2,1)S(1)}, bf16[2,1024,128]{2,1,0:T(8,128)(2,1)S(1)}, u32[]{:S(2)}, u32[]{:S(2)}) %collective-permute-start.27) | collective-permute-done | bytes 524320 | tf_op jit(solution)/shard_map/ppermute | solution.py:54
  487.8 37.2 %collective-permute-done.23 = bf16[2,1024,128]{2,1,0:T(8,128)(2,1)S(1)} collective-permute-done((bf16[2,1024,128]{2,1,0:T(8,128)(2,1)S(1)}, bf16[2,1024,128]{2,1,0:T(8,128)(2,1)S(1)}, u32[]{:S(2)}, u32[]{:S(2)}) %collective-permute-start.23) | collective-permute-done | bytes 524320 | tf_op jit(solution)/shard_map/ppermute | solution.py:54
  525.0 17.6 %collective-permute-start.50 = (bf16[2,2,24,768]{3,2,1,0:T(8,128)(2,1)S(1)}, bf16[2,2,24,768]{3,2,1,0:T(8,128)(2,1)S(1)}, u32[]{:S(2)}, u32[]{:S(2)}) collective-permute-start(bf16[2,2,24,768]{3,2,1,0:T(8,128)(2,1)S(1)} %fusion.77), channel_id=1, source_target_pairs={{0,2},{1,3},{2,0},{3,1},{4,6},{5,7},{6,4},{7,5},{8,10},{9,11},{10,... | collective-permute-start | bytes 442376 | tf_op jit(solution)/shard_map/ppermute | solution.py:59
  544.7 6.3 collective-permute-done.50
  551.8 22.6 %collective-permute-start.51 = (bf16[2,24,768]{2,1,0:T(8,128)(2,1)}, bf16[2,24,768]{2,1,0:T(8,128)(2,1)}, u32[]{:S(2)}, u32[]{:S(2)}) collective-permute-start(bf16[2,24,768]{2,1,0:T(8,128)(2,1)} %fusion.82), channel_id=1, source_target_pairs={{0,8},{1,9},{2,10},{3,11},{4,12},{5,13},{6,14},{7,15},{8,0},{9,1},... | collective-permute-start | bytes 221192 | tf_op jit(solution)/shard_map/ppermute | solution.py:59
  574.5 5.0 select_convert_fusion
  585.3 18.2 %collective-permute-start.52 = (bf16[24,768]{1,0:T(8,128)(2,1)}, bf16[24,768]{1,0:T(8,128)(2,1)}, u32[]{:S(2)}, u32[]{:S(2)}) collective-permute-start(bf16[24,768]{1,0:T(8,128)(2,1)} %fusion.86), channel_id=1, source_target_pairs={{0,16},{1,17},{2,18},{3,19},{4,20},{5,21},{6,22},{7,23},{8,24},{9,... | collective-permute-start | bytes 110600 | tf_op jit(solution)/shard_map/ppermute | solution.py:59
  643.7 29.2 %collective-permute-done.44 = bf16[2,2,2,24,1152]{4,3,0,1,2:T(8,128)(2,1)S(1)} collective-permute-done((bf16[2,2,2,24,1152]{4,3,0,1,2:T(8,128)(2,1)S(1)}, bf16[2,2,2,24,1152]{4,3,0,1,2:T(8,128)(2,1)S(1)}, u32[]{:S(2)}, u32[]{:S(2)}) %collective-permute-start.44) | collective-permute-done | bytes 442400 | tf_op jit(solution)/shard_map/ppermute | solution.py:59
  674.5 4.8 collective-permute-done.39
  701.8 7.5 %collective-permute-done.56 = bf16[2,24,3072]{2,1,0:T(8,128)(2,1)S(1)} collective-permute-done((bf16[2,24,3072]{2,1,0:T(8,128)(2,1)S(1)}, bf16[2,24,3072]{2,1,0:T(8,128)(2,1)S(1)}, u32[]{:S(2)}, u32[]{:S(2)}) %collective-permute-start.56) | collective-permute-done | bytes 294944 | tf_op jit(solution)/shard_map/ppermute | solution.py:59
  (581 shorter events, 243.6 us)
Async XLA Ops:
  7.2 66.6 %all-gather.5.cloned.1.call-start = ((), (), s32[]{:S(2)}) async-start(), calls=%async_computation | async-start | bytes 3649536 | tf_op jit(solution)/shard_map/all_gather | solution.py:285
  7.9 243.8 %all-gather.7.cloned.1.call-start = ((), (), s32[]{:S(2)}) async-start(), calls=%async_computation.1 | async-start | bytes 1216512 | tf_op jit(solution)/shard_map/all_gather | solution.py:286
  8.7 247.1 %all-gather.9.cloned.1.call-start = ((), (), s32[]{:S(2)}) async-start(), calls=%async_computation.2 | async-start | bytes 4866048 | tf_op jit(solution)/shard_map/all_gather | solution.py:287
  9.4 285.1 %all-gather.11.cloned.1.call-start = ((), (), s32[]{:S(2)}) async-start(), calls=%async_computation.3 | async-start | bytes 4866048 | tf_op jit(solution)/shard_map/all_gather | solution.py:288
  106.5 37.2 %collective-permute-start.15 = (bf16[2,1024,128]{2,1,0:T(8,128)(2,1)S(1)}, bf16[2,1024,128]{2,1,0:T(8,128)(2,1)S(1)}, u32[]{:S(2)}, u32[]{:S(2)}) collective-permute-start(bf16[2,1024,128]{2,1,0:T(8,128)(2,1)S(1)} %get-tuple-element.78.refs_0_), channel_id=1, source_target_pairs={{0,4},{1,5},{2,6},{3,7},{4,8},{5,9},{6,10},{7,11},{8,12},{9,13},{1... | collective-permute-start | bytes 1572872 | tf_op jit(solution)/shard_map/ppermute | solution.py:54
  109.2 38.6 %collective-permute-start.16 = (bf16[2,1024,128]{2,1,0:T(8,128)(2,1)S(1)}, bf16[2,1024,128]{2,1,0:T(8,128)(2,1)}, u32[]{:S(2)}, u32[]{:S(2)}) collective-permute-start(bf16[2,1024,128]{2,1,0:T(8,128)(2,1)S(1)} %get-tuple-element.78.refs_0_), channel_id=1, source_target_pairs={{0,6},{1,7},{2,8},{3,9},{4,10},{5,11},{6,12},{7,13},{8,14},{9,15},... | collective-permute-start | bytes 1572872 | tf_op jit(solution)/shard_map/ppermute | solution.py:54
  116.9 34.3 %collective-permute-start.17 = (bf16[2,1024,128]{2,1,0:T(8,128)(2,1)S(1)}, bf16[2,1024,128]{2,1,0:T(8,128)(2,1)}, u32[]{:S(2)}, u32[]{:S(2)}) collective-permute-start(bf16[2,1024,128]{2,1,0:T(8,128)(2,1)S(1)} %get-tuple-element.78.refs_0_), channel_id=1, source_target_pairs={{0,8},{1,9},{2,10},{3,11},{4,12},{5,13},{6,14},{7,15},{8,16},{9,17... | collective-permute-start | bytes 1572872 | tf_op jit(solution)/shard_map/ppermute | solution.py:54
  119.6 38.3 %collective-permute-start.10 = (bf16[2,1024,128]{2,1,0:T(8,128)(2,1)S(1)}, bf16[2,1024,128]{2,1,0:T(8,128)(2,1)S(1)}, u32[]{:S(2)}, u32[]{:S(2)}) collective-permute-start(bf16[2,1024,128]{2,1,0:T(8,128)(2,1)S(1)} %get-tuple-element.77.refs_0_), channel_id=1, source_target_pairs={{0,2},{1,3},{2,4},{3,5},{4,6},{5,7},{6,8},{7,9},{8,10},{9,11},{10,... | collective-permute-start | bytes 1572872 | tf_op jit(solution)/shard_map/ppermute | solution.py:54
  121.2 52.3 %collective-permute-start.11 = (bf16[2,1024,128]{2,1,0:T(8,128)(2,1)S(1)}, bf16[2,1024,128]{2,1,0:T(8,128)(2,1)}, u32[]{:S(2)}, u32[]{:S(2)}) collective-permute-start(bf16[2,1024,128]{2,1,0:T(8,128)(2,1)S(1)} %get-tuple-element.77.refs_0_), channel_id=1, source_target_pairs={{0,4},{1,5},{2,6},{3,7},{4,8},{5,9},{6,10},{7,11},{8,12},{9,13},{1... | collective-permute-start | bytes 1572872 | tf_op jit(solution)/shard_map/ppermute | solution.py:54
  144.5 66.6 %collective-permute-start.12 = (bf16[2,1024,128]{2,1,0:T(8,128)(2,1)S(1)}, bf16[2,1024,128]{2,1,0:T(8,128)(2,1)}, u32[]{:S(2)}, u32[]{:S(2)}) collective-permute-start(bf16[2,1024,128]{2,1,0:T(8,128)(2,1)S(1)} %get-tuple-element.77.refs_0_), channel_id=1, source_target_pairs={{0,6},{1,7},{2,8},{3,9},{4,10},{5,11},{6,12},{7,13},{8,14},{9,15},... | collective-permute-start | bytes 1572872 | tf_op jit(solution)/shard_map/ppermute | solution.py:54
  147.9 71.7 %collective-permute-start.13 = (bf16[2,1024,128]{2,1,0:T(8,128)(2,1)S(1)}, bf16[2,1024,128]{2,1,0:T(8,128)(2,1)S(1)}, u32[]{:S(2)}, u32[]{:S(2)}) collective-permute-start(bf16[2,1024,128]{2,1,0:T(8,128)(2,1)S(1)} %get-tuple-element.77.refs_0_), channel_id=1, source_target_pairs={{0,8},{1,9},{2,10},{3,11},{4,12},{5,13},{6,14},{7,15},{8,16},{9,17... | collective-permute-start | bytes 1572872 | tf_op jit(solution)/shard_map/ppermute | solution.py:54
  151.2 76.8 %collective-permute-start.6 = (bf16[2,1024,128]{2,1,0:T(8,128)(2,1)S(1)}, bf16[2,1024,128]{2,1,0:T(8,128)(2,1)S(1)}, u32[]{:S(2)}, u32[]{:S(2)}) collective-permute-start(bf16[2,1024,128]{2,1,0:T(8,128)(2,1)S(1)} %get-tuple-element.76.refs_0_), channel_id=1, source_target_pairs={{0,2},{1,3},{2,4},{3,5},{4,6},{5,7},{6,8},{7,9},{8,10},{9,11},{10,... | collective-permute-start | bytes 1572872 | tf_op jit(solution)/shard_map/ppermute | solution.py:54
  158.7 69.3 %collective-permute-start.7 = (bf16[2,1024,128]{2,1,0:T(8,128)(2,1)S(1)}, bf16[2,1024,128]{2,1,0:T(8,128)(2,1)S(1)}, u32[]{:S(2)}, u32[]{:S(2)}) collective-permute-start(bf16[2,1024,128]{2,1,0:T(8,128)(2,1)S(1)} %get-tuple-element.76.refs_0_), channel_id=1, source_target_pairs={{0,4},{1,5},{2,6},{3,7},{4,8},{5,9},{6,10},{7,11},{8,12},{9,13},{1... | collective-permute-start | bytes 1572872 | tf_op jit(solution)/shard_map/ppermute | solution.py:54
  173.4 54.6 %collective-permute-start.8 = (bf16[2,1024,128]{2,1,0:T(8,128)(2,1)S(1)}, bf16[2,1024,128]{2,1,0:T(8,128)(2,1)S(1)}, u32[]{:S(2)}, u32[]{:S(2)}) collective-permute-start(bf16[2,1024,128]{2,1,0:T(8,128)(2,1)S(1)} %get-tuple-element.76.refs_0_), channel_id=1, source_target_pairs={{0,6},{1,7},{2,8},{3,9},{4,10},{5,11},{6,12},{7,13},{8,14},{9,15},... | collective-permute-start | bytes 1572872 | tf_op jit(solution)/shard_map/ppermute | solution.py:54
  330.8 50.7 %collective-permute-start.48 = (bf16[2,2,2,2,24,768]{5,4,3,2,1,0:T(8,128)(2,1)}, bf16[2,2,2,2,24,768]{5,4,3,2,1,0:T(8,128)(2,1)}, u32[]{:S(2)}, u32[]{:S(2)}) collective-permute-start(bf16[2,2,2,2,24,768]{5,4,3,2,1,0:T(8,128)(2,1)} %fusion.53), channel_id=1, source_target_pairs={{0,1},{1,0},{2,3},{3,2},{4,5},{5,4},{6,7},{7,6},{8,9},{9,8},{10,11... | collective-permute-start | bytes 1769480 | tf_op jit(solution)/shard_map/ppermute | solution.py:59
  358.0 95.9 %collective-permute-start.31 = (bf16[2,1024,128]{2,1,0:T(8,128)(2,1)}, bf16[2,1024,128]{2,1,0:T(8,128)(2,1)}, u32[]{:S(2)}, u32[]{:S(2)}) collective-permute-start(bf16[2,1024,128]{2,1,0:T(8,128)(2,1)} %get-tuple-element.71), channel_id=1, source_target_pairs={{8,0},{9,1},{10,2},{11,3},{12,4},{13,5},{14,6},{15,7},{16,8},{17,9... | collective-permute-start | bytes 1572872 | tf_op jit(solution)/shard_map/ppermute | solution.py:54
  359.4 95.8 %collective-permute-start.30 = (bf16[2,1024,128]{2,1,0:T(8,128)(2,1)}, bf16[2,1024,128]{2,1,0:T(8,128)(2,1)}, u32[]{:S(2)}, u32[]{:S(2)}) collective-permute-start(bf16[2,1024,128]{2,1,0:T(8,128)(2,1)} %get-tuple-element.72), channel_id=1, source_target_pairs={{6,0},{7,1},{8,2},{9,3},{10,4},{11,5},{12,6},{13,7},{14,8},{15,9},... | collective-permute-start | bytes 1572872 | tf_op jit(solution)/shard_map/ppermute | solution.py:54
  360.7 96.8 %collective-permute-start.29 = (bf16[2,1024,128]{2,1,0:T(8,128)(2,1)}, bf16[2,1024,128]{2,1,0:T(8,128)(2,1)}, u32[]{:S(2)}, u32[]{:S(2)}) collective-permute-start(bf16[2,1024,128]{2,1,0:T(8,128)(2,1)} %get-tuple-element.73), channel_id=1, source_target_pairs={{4,0},{5,1},{6,2},{7,3},{8,4},{9,5},{10,6},{11,7},{12,8},{13,9},{1... | collective-permute-start | bytes 1572872 | tf_op jit(solution)/shard_map/ppermute | solution.py:54
  362.0 97.2 %collective-permute-start.28 = (bf16[2,1024,128]{2,1,0:T(8,128)(2,1)}, bf16[2,1024,128]{2,1,0:T(8,128)(2,1)}, u32[]{:S(2)}, u32[]{:S(2)}) collective-permute-start(bf16[2,1024,128]{2,1,0:T(8,128)(2,1)} %get-tuple-element.70), channel_id=1, source_target_pairs={{2,0},{3,1},{4,2},{5,3},{6,4},{7,5},{8,6},{9,7},{10,8},{11,9},{12,... | collective-permute-start | bytes 1572872 | tf_op jit(solution)/shard_map/ppermute | solution.py:54
  382.9 69.7 %collective-permute-start.49 = (bf16[2,2,2,24,768]{4,3,2,1,0:T(8,128)(2,1)S(1)}, bf16[2,2,2,24,768]{4,3,2,1,0:T(8,128)(2,1)S(1)}, u32[]{:S(2)}, u32[]{:S(2)}) collective-permute-start(bf16[2,2,2,24,768]{4,3,2,1,0:T(8,128)(2,1)S(1)} %fusion.68), channel_id=1, source_target_pairs={{0,4},{1,5},{2,6},{3,7},{4,0},{5,1},{6,2},{7,3},{8,12},{9,13},{10,... | collective-permute-start | bytes 884744 | tf_op jit(solution)/shard_map/ppermute | solution.py:59
  459.2 65.8 %collective-permute-start.23 = (bf16[2,1024,128]{2,1,0:T(8,128)(2,1)S(1)}, bf16[2,1024,128]{2,1,0:T(8,128)(2,1)S(1)}, u32[]{:S(2)}, u32[]{:S(2)}) collective-permute-start(bf16[2,1024,128]{2,1,0:T(8,128)(2,1)S(1)} %get-tuple-element.63), channel_id=1, source_target_pairs={{8,0},{9,1},{10,2},{11,3},{12,4},{13,5},{14,6},{15,7},{16,8},{17,9... | collective-permute-start | bytes 1572872 | tf_op jit(solution)/shard_map/ppermute | solution.py:54
  480.0 44.9 %collective-permute-start.22 = (bf16[2,1024,128]{2,1,0:T(8,128)(2,1)S(1)}, bf16[2,1024,128]{2,1,0:T(8,128)(2,1)S(1)}, u32[]{:S(2)}, u32[]{:S(2)}) collective-permute-start(bf16[2,1024,128]{2,1,0:T(8,128)(2,1)S(1)} %get-tuple-element.64), channel_id=1, source_target_pairs={{6,0},{7,1},{8,2},{9,3},{10,4},{11,5},{12,6},{13,7},{14,8},{15,9},... | collective-permute-start | bytes 1572872 | tf_op jit(solution)/shard_map/ppermute | solution.py:54
  481.3 61.3 %collective-permute-start.21 = (bf16[2,1024,128]{2,1,0:T(8,128)(2,1)S(1)}, bf16[2,1024,128]{2,1,0:T(8,128)(2,1)S(1)}, u32[]{:S(2)}, u32[]{:S(2)}) collective-permute-start(bf16[2,1024,128]{2,1,0:T(8,128)(2,1)S(1)} %get-tuple-element.65), channel_id=1, source_target_pairs={{4,0},{5,1},{6,2},{7,3},{8,4},{9,5},{10,6},{11,7},{12,8},{13,9},{1... | collective-permute-start | bytes 1572872 | tf_op jit(solution)/shard_map/ppermute | solution.py:54
  483.5 59.2 %collective-permute-start.20 = (bf16[2,1024,128]{2,1,0:T(8,128)(2,1)S(1)}, bf16[2,1024,128]{2,1,0:T(8,128)(2,1)S(1)}, u32[]{:S(2)}, u32[]{:S(2)}) collective-permute-start(bf16[2,1024,128]{2,1,0:T(8,128)(2,1)S(1)} %get-tuple-element.62), channel_id=1, source_target_pairs={{2,0},{3,1},{4,2},{5,3},{6,4},{7,5},{8,6},{9,7},{10,8},{11,9},{12,... | collective-permute-start | bytes 1572872 | tf_op jit(solution)/shard_map/ppermute | solution.py:54
  487.3 145.0 %collective-permute-start.53 = (bf16[2,2,2,2,24,3072]{5,4,0,1,3,2:T(8,128)(2,1)}, bf16[2,2,2,2,24,3072]{5,4,0,1,3,2:T(8,128)(2,1)}, u32[]{:S(2)}, u32[]{:S(2)}) collective-permute-start(bf16[2,2,2,2,24,3072]{5,4,0,1,3,2:T(8,128)(2,1)} %fusion.11), channel_id=1, source_target_pairs={{0,1},{1,0},{2,3},{3,2},{4,5},{5,4},{6,7},{7,6},{8,9},{9,8},{10,11... | collective-permute-start | bytes 7077896 | tf_op jit(solution)/shard_map/ppermute | solution.py:59
  525.0 113.4 %collective-permute-start.58 = (bf16[2,2,2,2,96,768]{5,4,0,1,2,3:T(8,128)(2,1)}, bf16[2,2,2,2,96,768]{5,4,0,1,2,3:T(8,128)(2,1)}, u32[]{:S(2)}, u32[]{:S(2)}) collective-permute-start(bf16[2,2,2,2,96,768]{5,4,0,1,2,3:T(8,128)(2,1)} %fusion.12), channel_id=1, source_target_pairs={{0,1},{1,0},{2,3},{3,2},{4,5},{5,4},{6,7},{7,6},{8,9},{9,8},{10,11... | collective-permute-start | bytes 7077896 | tf_op jit(solution)/shard_map/ppermute | solution.py:59
  544.4 59.0 %collective-permute-start.32 = (bf16[3,512,384]{2,1,0:T(8,128)(2,1)}, bf16[3,512,384]{2,1,0:T(8,128)(2,1)S(1)}, u32[]{:S(2)}, u32[]{:S(2)}) collective-permute-start(bf16[3,512,384]{2,1,0:T(8,128)(2,1)} %constant_dynamic-slice_fusion.16), channel_id=1, source_target_pairs={{0,1},{1,0},{2,3},{3,2},{4,5},{5,4},{6,7},{7,6},{8,9},{9,8},{10,11... | collective-permute-start | bytes 3538952 | tf_op jit(solution)/shard_map/ppermute | solution.py:59
  551.8 31.9 %collective-permute-start.51 = (bf16[2,24,768]{2,1,0:T(8,128)(2,1)}, bf16[2,24,768]{2,1,0:T(8,128)(2,1)}, u32[]{:S(2)}, u32[]{:S(2)}) collective-permute-start(bf16[2,24,768]{2,1,0:T(8,128)(2,1)} %fusion.82), channel_id=1, source_target_pairs={{0,8},{1,9},{2,10},{3,11},{4,12},{5,13},{6,14},{7,15},{8,0},{9,1},... | collective-permute-start | bytes 221192 | tf_op jit(solution)/shard_map/ppermute | solution.py:59
  636.3 43.3 %collective-permute-start.54 = (bf16[2,2,2,24,3072]{4,3,0,1,2:T(8,128)(2,1)S(1)}, bf16[2,2,2,24,3072]{4,3,0,1,2:T(8,128)(2,1)S(1)}, u32[]{:S(2)}, u32[]{:S(2)}) collective-permute-start(bf16[2,2,2,24,3072]{4,3,0,1,2:T(8,128)(2,1)S(1)} %fusion.25), channel_id=1, source_target_pairs={{0,4},{1,5},{2,6},{3,7},{4,0},{5,1},{6,2},{7,3},{8,12},{9,13},{10,... | collective-permute-start | bytes 3538952 | tf_op jit(solution)/shard_map/ppermute | solution.py:59
  640.9 40.5 %collective-permute-start.59 = (bf16[2,2,2,96,768]{4,3,0,1,2:T(8,128)(2,1)S(1)}, bf16[2,2,2,96,768]{4,3,0,1,2:T(8,128)(2,1)S(1)}, u32[]{:S(2)}, u32[]{:S(2)}) collective-permute-start(bf16[2,2,2,96,768]{4,3,0,1,2:T(8,128)(2,1)S(1)} %fusion.26), channel_id=1, source_target_pairs={{0,2},{1,3},{2,0},{3,1},{4,6},{5,7},{6,4},{7,5},{8,10},{9,11},{10,... | collective-permute-start | bytes 3538952 | tf_op jit(solution)/shard_map/ppermute | solution.py:59
  642.6 30.4 %collective-permute-start.44 = (bf16[2,2,2,24,1152]{4,3,0,1,2:T(8,128)(2,1)S(1)}, bf16[2,2,2,24,1152]{4,3,0,1,2:T(8,128)(2,1)S(1)}, u32[]{:S(2)}, u32[]{:S(2)}) collective-permute-start(bf16[2,2,2,24,1152]{4,3,0,1,2:T(8,128)(2,1)S(1)} %fusion.61), channel_id=1, source_target_pairs={{0,4},{1,5},{2,6},{3,7},{4,0},{5,1},{6,2},{7,3},{8,12},{9,13},{10,... | collective-permute-start | bytes 1327112 | tf_op jit(solution)/shard_map/ppermute | solution.py:59
  643.0 36.4 %collective-permute-start.39 = (bf16[2,2,2,24,1152]{4,3,0,1,2:T(8,128)(2,1)S(1)}, bf16[2,2,2,24,1152]{4,3,0,1,2:T(8,128)(2,1)S(1)}, u32[]{:S(2)}, u32[]{:S(2)}) collective-permute-start(bf16[2,2,2,24,1152]{4,3,0,1,2:T(8,128)(2,1)S(1)} %fusion.60), channel_id=1, source_target_pairs={{0,2},{1,3},{2,0},{3,1},{4,6},{5,7},{6,4},{7,5},{8,10},{9,11},{10,... | collective-permute-start | bytes 1327112 | tf_op jit(solution)/shard_map/ppermute | solution.py:59
  (161 other events, 3069.6 us)
Sparse Core Ops, SparseCore 0:
  10.9 62.7 all-gather.4
  76.7 65.8 all-gather.6
  145.4 74.8 all-gather.8
  223.1 71.3 all-gather.10
